TPU v7x, 256 devices: a whole 4x4x8 slice. The times are simulated.
256 devices in a mesh: px: 64 (over y_lo, z, x), py: 4 (over y_hi, core).
Axes of the slice: x: 4, y: 4 (y_hi: 2, y_lo: 2; y = y_hi * 2 + y_lo), z: 8, core: 2. Of those that a mesh axis runs over, the one named last changes fastest.
Arguments:
- features: bfloat16 [64, 128, 128, 128], P(None, 'px', 'py'), may hold values from -6 to 6
- cotangent: bfloat16 [64, 128, 128, 128], P(None, 'px', 'py'), may hold values from -6 to 6
- tucker_core: bfloat16 [2304, 2048], replicated, may hold values from -6 to 6
- in_factor: float32 [64, 48], replicated, may hold values from -0.875 to 0.875
- out_factor: float32 [64, 48], replicated, may hold values from -0.875 to 0.875
- x_factor: float32 [32, 16], replicated, may hold values from -1.5 to 1.5
- y_factor: float32 [32, 16], replicated, may hold values from -1.5 to 1.5
- z_factor: float32 [16, 8], replicated, may hold values from -2 to 2
Outputs:
- grad_features: bfloat16 [64, 128, 128, 128], P(None, 'px', 'py')
- grad_core: float32 [2304, 2048], P(('px', 'py'))
- grad_in: float32 [64, 48], replicated
- grad_out: float32 [64, 48], replicated
- grad_x: float32 [32, 16], replicated
- grad_y: float32 [32, 16], replicated
- grad_z: float32 [16, 8], replicated
All inputs are finite; a program needn't handle non-finite values.
Results may differ from a plain program's by a relative error of at most 0.015.
Values may be sent and summed in bfloat16 or wider, within the bound.
A program may use at most 128 MiB of HBM per device.

v0:
```python
import math

import jax
import jax.numpy as jnp
from jax import lax
from jax.sharding import PartitionSpec as P

NX = 128
NY = 128
NZ = 128
KX = 32
KY = 32
KZ = 16
RIN = 48
ROUT = 48
RX = 16
RY = 16
RZ = 8


precise = lax.Precision.HIGHEST


def fourier_rows(count, length, offset, width):
    half = count // 2
    row_ids = lax.broadcasted_iota(jnp.int32, (count, width), 0)
    col_ids = lax.broadcasted_iota(jnp.int32, (count, width), 1) + offset
    freq = jnp.where(row_ids < half, row_ids, row_ids - half + 1)
    phase = freq * col_ids % length
    angle = phase.astype(jnp.float32) * (2.0 * math.pi / length)
    return jnp.where(row_ids < half, jnp.cos(angle), jnp.sin(angle)) * math.sqrt(2.0 / length)


def pair_outer(within, y_offset, fy, fz, pair_total):
    y_mode = y_offset + within // KZ
    z_mode = within % KZ
    pick_y = (y_mode[:, None] == lax.broadcasted_iota(jnp.int32, (pair_total, KY), 1)).astype(
        jnp.float32
    )
    pick_z = (z_mode[:, None] == lax.broadcasted_iota(jnp.int32, (pair_total, KZ), 1)).astype(
        jnp.float32
    )
    y_rows = jnp.dot(pick_y, fy, precision=precise)
    z_rows = jnp.dot(pick_z, fz, precision=precise)
    return (y_rows[:, :, None] * z_rows[:, None, :]).reshape(pair_total, RY * RZ)


def shards(features, cotangent, tucker_core, in_factor, out_factor, x_factor, y_factor, z_factor):
    channels, planes, strip_len, depth = features.shape
    px_count = lax.axis_size("px")
    py_count = lax.axis_size("py")
    px_id = lax.axis_index("px")
    py_id = lax.axis_index("py")
    ky_local = KY // py_count
    pair_count = ky_local * KZ // px_count
    z_basis = fourier_rows(KZ, NZ, 0, NZ)
    y_basis = fourier_rows(KY, NY, py_id * strip_len, strip_len)
    x_basis = fourier_rows(KX, NX, 0, NX).reshape(KX, px_count, planes)
    z_input = jnp.einsum("cxyz,kz->cxyk", features, z_basis, precision=precise)
    z_cotan = jnp.einsum("cxyz,kz->cxyk", cotangent, z_basis, precision=precise)
    basis_rows = y_basis
    term_in = jnp.einsum("cxyk,jy->jkxc", z_input, basis_rows, precision=precise)
    term_out = jnp.einsum("cxyk,jy->jkxc", z_cotan, basis_rows, precision=precise)
    summed = lax.psum_scatter(
        jnp.concatenate(
            [
                term_in.reshape(ky_local * lax.axis_size("py"), KZ, planes * channels),
                term_out.reshape(ky_local * lax.axis_size("py"), KZ, planes * channels),
            ],
            axis=2,
        ),
        "py",
        scatter_dimension=0,
        tiled=True,
    )
    packed = summed.astype(jnp.bfloat16).reshape(ky_local * KZ, 2 * planes * channels)
    owner_data = lax.all_to_all(packed, "px", split_axis=0, concat_axis=1, tiled=True)
    owner_data = owner_data.reshape(pair_count, px_count, 2, planes, channels)
    spectra = jnp.einsum("npwdc,apd->wanc", owner_data, x_basis, precision=precise)
    spec_in = spectra[0]
    spec_out = spectra[1]
    within = px_id * pair_count + lax.broadcasted_iota(jnp.int32, (pair_count,), 0)
    core_matrix = tucker_core.reshape(RIN * ROUT * RX, RY * RZ)

    def outer_fn(fy, fz):
        return pair_outer(within, py_id * ky_local, fy, fz, pair_count)

    yz_outer, pull_outer = jax.vjp(outer_fn, y_factor, z_factor)
    core_pairs = jnp.dot(core_matrix, yz_outer.T, precision=precise)

    def expand(core_cols, fin, fout, fx):
        reshaped = core_cols.reshape(RIN, ROUT, RX, pair_count)
        section = jnp.einsum("pqrn,ar->pqan", reshaped, fx, precision=precise)
        section = jnp.einsum("pqan,ip->iqan", section, fin, precision=precise)
        return jnp.einsum("iqan,oq->anio", section, fout, precision=precise)

    weight, pull_expand = jax.vjp(expand, core_pairs, in_factor, out_factor, x_factor)
    grad_weight = spec_in[:, :, :, None] * spec_out[:, :, None, :]
    core_flow, grad_in, grad_out, grad_x = pull_expand(grad_weight)
    grad_outer = jnp.dot(core_flow.T, core_matrix, precision=precise)
    grad_y, grad_z = pull_outer(grad_outer)
    pulled = jnp.einsum("anio,ano->ani", weight, spec_out, precision=precise)
    x_synth = jnp.einsum("ani,apd->npdi", pulled, x_basis, precision=precise).astype(jnp.bfloat16)
    x_synth = x_synth.reshape(pair_count, px_count * planes * channels)
    returned = lax.all_to_all(x_synth, "px", split_axis=1, concat_axis=0, tiled=True)
    returned = returned.reshape(ky_local, KZ, planes, channels)
    basis_rows = y_basis
    y_summed = jnp.einsum(
        "jkxc,jy->cxyk",
        lax.all_gather(returned, "py", axis=0, tiled=True),
        basis_rows,
        precision=precise,
    )
    grad_features = jnp.einsum("cxyk,kz->cxyz", y_summed, z_basis, precision=precise).astype(
        jnp.bfloat16
    )
    factor_grads = lax.psum((grad_in, grad_out, grad_x, grad_y, grad_z), ("px", "py"))
    core_flow = core_flow.reshape(RIN * ROUT, RX, pair_count)
    shard_rows = RIN * ROUT // (px_count * py_count)
    gathered = lax.all_to_all(
        core_flow.astype(jnp.bfloat16), "px", split_axis=0, concat_axis=2, tiled=True
    ).astype(core_flow.dtype)
    group_pairs = lax.broadcasted_iota(jnp.int32, (ky_local * KZ,), 0)
    group_outer = pair_outer(group_pairs, py_id * ky_local, y_factor, z_factor, ky_local * KZ)
    grad_core = lax.psum_scatter(
        jnp.einsum("mrn,ns->mrs", gathered, group_outer, precision=precise)
        .reshape(shard_rows * lax.axis_size("py"), RX * RY * RZ)
        .astype(jnp.bfloat16),
        "py",
        scatter_dimension=0,
        tiled=True,
    ).astype(jnp.float32)
    return (
        grad_features,
        grad_core,
        factor_grads[0],
        factor_grads[1],
        factor_grads[2],
        factor_grads[3],
        factor_grads[4],
    )


def solution(mesh):
    placed = (P(None, "px", "py", None), P(None, "px", "py", None), P(), P(), P(), P(), P(), P())
    return jax.shard_map(
        shards,
        mesh=mesh,
        in_specs=placed,
        out_specs=(P(None, "px", "py", None), P(("px", "py"), None), P(), P(), P(), P(), P()),
        check_vma=False,
    )
```

profile of v0, /device:TPU:1, one launch (start us, length us, event | category | flops | bytes accessed | tf_op | source)
XLA Modules:
  0.0 363.1 jit_solution(13645452248143948360)
XLA Ops:
  8.4 2.6 convolution_bitcast_fusion.5
  12.6 2.6 convolution_bitcast_fusion.6
  19.6 35.8 %reduce-scatter.2.cloned.1.call-done = f32[8,16,256]{2,1,0:T(8,128)} async-done(((f32[32,16,256]{2,1,0:T(8,128)}), f32[8,16,256]{2,1,0:T(8,128)}) %reduce-scatter.2.cloned.1.call-update) | async-done | bytes 131088 | tf_op jit(solution)/shard_map/reduce_scatter | solution.py:64
  57.0 10.4 %all-to-all-start = ((bf16[64,2,256]{2,1,0:T(2,128)(2,1)}), bf16[64,2,256]{2,1,0:T(2,128)(2,1)S(1)}, u32[]{:S(2)}, u32[]{:S(2)}) async-start(bf16[64,2,256]{2,1,0:T(2,128)(2,1)} %all_to_all.37), calls=%async_computation.1 | async-start | bytes 131072 | tf_op jit(solution)/shard_map/all_to_all | solution.py:77
  68.2 15.0 %reshape.172 = bf16[36864,128]{1,0:T(8,128)(2,1)} reshape(bf16[2304,2048]{1,0:T(8,128)(2,1)} %param.10) | data formatting | bytes 18874368 | tf_op jit(solution)/shard_map/reshape | solution.py:83
  83.2 12.6 %copy.110 = bf16[128,36864]{1,0:T(8,128)(2,1)} copy(bf16[128,36864]{0,1:T(8,128)(2,1)} %bitcast.168) | data formatting | bytes 18874368 | tf_op jit(solution)/shard_map/dot_general | solution.py:100
  97.7 2.2 fusion.4
  101.1 2.5 fusion.19
  103.6 2.8 copy.99
  106.5 1.7 fusion.135
  108.1 2.1 copy.109
  110.3 2.9 reshape.196
  113.2 36.5 %multiply_reduce_fusion = (f32[2,8]{0,1:T(8,128)}, f32[2,16]{1,0:T(2,128)}, f32[2,16,8]{1,0,2:T(2,128)S(1)}) fusion(f32[2,16]{1,0:T(2,128)S(1)} %copy-done.32, f32[2,8]{0,1:T(8,128)S(1)} %copy-done.30, f32[36864,2,1]{0,1,2:T(2,128)S(1)} %reshape.196, bf16[16,8,36864]{2,1,0:T(8,128)(2,1)} %bitcast.169), kind=kOutput, calls=%fused_computation.100 | convolution fusion | flops 113247440 | bytes 9733504 | tf_op jit(solution)/shard_map/dot_general | solution.py:100
  149.9 10.7 %convolution_bitcast_fusion = f32[36864,2]{0,1:T(2,128)} fusion(f32[2,128]{1,0:T(2,128)S(1)} %mul.170, bf16[36864,128]{1,0:T(8,128)(2,1)} %reshape.172), kind=kOutput, calls=%fused_computation | convolution fusion | flops 113246208 | bytes 9733120 | tf_op jit(solution)/shard_map/dot_general | solution.py:89
  160.5 1.8 reshape.173
  162.3 5.2 %fusion.39 = f32[32,16]{0,1:T(8,128)S(1)} fusion(f32[32,48,48,2]{2,0,3,1:T(8,128)} %copy-done.1, f32[48,48,16,2]{2,1,0,3:T(8,128)S(1)} %reshape.173), kind=kOutput, calls=%fused_computation.38 | convolution fusion | flops 28311552 | bytes 886784 | tf_op jit(solution)/shard_map/transpose(jvp(pqrn,ar->pqan))/dot_general | solution.py:93
  167.5 7.9 %fusion.22 = f32[48,48,32,2]{1,2,3,0:T(8,128)S(1)} fusion(f32[48,48,16,2]{2,1,0,3:T(8,128)S(1)} %reshape.173, f32[32,16]{0,1:T(8,128)S(1)} %copy-done.7), kind=kOutput, calls=%fused_computation.21 | convolution fusion | flops 28311552 | bytes 886784 | tf_op jit(solution)/shard_map/jvp(pqrn,ar->pqan)/dot_general | solution.py:93
  175.4 3.3 fusion.29
  178.9 3.9 %fusion.25 = f32[48,32,2,64]{3,0,2,1:T(8,128)S(1)} fusion(f32[48,48,32,2]{1,2,3,0:T(8,128)S(1)} %fusion.22, f32[64,48]{0,1:T(8,128)S(1)} %copy-done.6), kind=kOutput, calls=%fused_computation.23 | convolution fusion | flops 113246208 | bytes 1388544 | tf_op jit(solution)/shard_map/jvp(pqan,ip->iqan)/dot_general | solution.py:94
  183.2 3.5 fusion.17
  186.7 3.3 fusion.10
  191.4 11.1 %all-to-all-start.1 = ((bf16[2,64,128]{2,0,1:T(2,128)(2,1)}), bf16[2,64,128]{2,0,1:T(2,128)(2,1)S(1)}, u32[]{:S(2)}, u32[]{:S(2)}) async-start(bf16[2,64,128]{2,0,1:T(2,128)(2,1)} %reshape.198), calls=%async_computation.2 | async-start | bytes 65536 | tf_op jit(solution)/shard_map/all_to_all | solution.py:105
  202.5 2.0 fusion.34
  205.4 2.0 reshape.201
  207.4 77.6 %all-reduce.1 = (f32[64,48]{0,1:T(8,128)}, f32[64,48]{0,1:T(8,128)}, f32[32,16]{0,1:T(8,128)}, f32[32,16]{0,1:T(8,128)}, f32[16,8]{0,1:T(8,128)}) all-reduce(f32[64,48]{0,1:T(8,128)S(1)} %fusion.29, f32[64,48]{0,1:T(8,128)S(1)} %fusion.34, f32[32,16]{0,1:T(8,128)S(1)} %fusion.39, ...), channel_id=1, replica_groups=mesh['px'=64,'py'=4] {'px','py'}, use_global_device_ids=true, to_apply=%region_2.3 | all-reduce | flops 7296 | bytes 58368 | tf_op jit(solution)/shard_map/psum | solution.py:117
  284.9 7.8 %all-to-all-start.2 = ((bf16[64,2,576]{2,1,0:T(2,128)(2,1)}), bf16[64,2,576]{2,1,0:T(2,128)(2,1)S(1)}, u32[]{:S(2)}, u32[]{:S(2)}) async-start(bf16[64,2,576]{2,1,0:T(2,128)(2,1)} %reshape.201), calls=%async_computation.3 | async-start | bytes 327680 | tf_op jit(solution)/shard_map/all_to_all | solution.py:120
  293.0 8.5 %all_gather.3 = bf16[32,16,2,64]{3,0,2,1:T(8,128)(2,1)S(1)} all-gather(bf16[8,16,2,64]{3,0,2,1:T(8,128)(2,1)S(1)} %copy.95), channel_id=1, replica_groups=mesh['px'=64,'py'=4] {'py'}, dimensions={0}, use_global_device_ids=true | all-gather | bytes 163840 | tf_op jit(solution)/shard_map/all_gather | solution.py:110
  303.8 2.5 copy.139
  306.3 1.6 copy.104
  308.9 4.5 %convolution_convert_fusion = bf16[64,2,32,128]{3,2,1,0:T(8,128)(2,1)} fusion(f32[64,2,32,16]{2,3,1,0:T(8,128)S(1)} %copy.96, s32[16]{0:T(128)S(1)} %copy-done.19, pred[16]{0:T(512)(128)(4,1)S(1)} %copy-done.17), kind=kOutput, calls=%fused_computation.22 | convolution fusion | flops 101222400 | bytes 1310800 | tf_op jit(solution)/shard_map/cxyk,kz->cxyz/dot_general | solution.py:114
  313.4 40.8 %all-reduce.4.cloned.1.call-done = bf16[36,2048]{1,0:T(8,128)(2,1)} async-done(((bf16[36,2048]{1,0:T(8,128)(2,1)}), bf16[36,2048]{1,0:T(8,128)(2,1)}) %all-reduce.4.cloned.1.call-update) | async-done | bytes 147472
  354.2 1.6 dynamic-slice_convert_fusion
  (118 shorter events, 17.9 us)
Async XLA Ops:
  7.2 48.2 %reduce-scatter.2.cloned.1.call-start = ((), (), s32[]{:S(2)}) async-start(), calls=%async_computation.4 | async-start | bytes 655360 | tf_op jit(solution)/shard_map/reduce_scatter | solution.py:64
  7.2 90.0 %copy-start.10 = (pred[32]{0:T(512)(128)(4,1)}, pred[32]{0:T(512)(128)(4,1)S(1)}, u32[]{:S(2)}) copy-start(pred[32]{0:T(512)(128)(4,1)S(1)} %iota_compare_fusion.11) | copy-start | bytes 100
  7.3 5.3 %copy-start.16 = (pred[16]{0:T(512)(128)(4,1)}, pred[16]{0:T(512)(128)(4,1)S(1)}, u32[]{:S(2)}) copy-start(pred[16]{0:T(512)(128)(4,1)S(1)} %iota_compare_fusion.10) | copy-start | bytes 52
  7.3 5.3 %copy-start.18 = (s32[16]{0:T(128)}, s32[16]{0:T(128)S(1)}, u32[]{:S(2)}) copy-start(s32[16]{0:T(128)S(1)} %iota_add_fusion) | copy-start | bytes 196
  8.4 6.9 %copy-start.12 = (s32[32]{0:T(128)}, s32[32]{0:T(128)S(1)}, u32[]{:S(2)}) copy-start(s32[32]{0:T(128)S(1)} %get-tuple-element.22) | copy-start | bytes 388
  8.4 88.8 %copy-start.14 = (s32[32]{0:T(128)}, s32[32]{0:T(128)S(1)}, u32[]{:S(2)}) copy-start(s32[32]{0:T(128)S(1)} %get-tuple-element.23) | copy-start | bytes 388
  17.8 65.4 %copy-start.23 = (s32[2]{0:T(128)}, s32[2]{0:T(128)S(1)}, u32[]{:S(2)}) copy-start(s32[2]{0:T(128)S(1)} %get-tuple-element.20) | copy-start | bytes 28
  57.0 40.1 %all-to-all-start = ((bf16[64,2,256]{2,1,0:T(2,128)(2,1)}), bf16[64,2,256]{2,1,0:T(2,128)(2,1)S(1)}, u32[]{:S(2)}, u32[]{:S(2)}) async-start(bf16[64,2,256]{2,1,0:T(2,128)(2,1)} %all_to_all.37), calls=%async_computation.1 | async-start | bytes 131072 | tf_op jit(solution)/shard_map/all_to_all | solution.py:77
  83.2 12.6 %copy-start.27 = (u32[256]{0:T(256)S(1)}, u32[256]{0:T(256)}, u32[]{:S(2)}) copy-start(u32[256]{0:T(256)} %constant.121) | copy-start | bytes 3076
  83.2 14.6 %copy-start.8 = (f32[64,48]{0,1:T(8,128)S(1)}, f32[64,48]{0,1:T(8,128)}, u32[]{:S(2)}) copy-start(f32[64,48]{0,1:T(8,128)} %param.12) | copy-start | bytes 36868
  95.8 5.3 %copy-start.6 = (f32[64,48]{0,1:T(8,128)S(1)}, f32[64,48]{0,1:T(8,128)}, u32[]{:S(2)}) copy-start(f32[64,48]{0,1:T(8,128)} %param.11) | copy-start | bytes 36868
  97.1 6.6 %copy-start.28 = (s32[64,2]{0,1:T(2,128)}, s32[64,2]{0,1:T(2,128)S(1)}, u32[]{:S(2)}) copy-start(s32[64,2]{0,1:T(2,128)S(1)} %multiply_add_fusion) | copy-start | bytes 1540
  106.4 3.8 %copy-start.1 = (f32[32,48,48,2]{2,0,3,1:T(8,128)}, f32[32,48,48,2]{2,0,3,1:T(8,128)S(1)}, u32[]{:S(2)}) copy-start(f32[32,48,48,2]{2,0,3,1:T(8,128)S(1)} %copy.99) | copy-start | bytes 1769476
  110.3 2.9 copy-start.30
  110.3 2.9 copy-start.32
  167.5 7.9 %copy-start.3 = (f32[64,32,2,48]{0,3,2,1:T(8,128)S(1)}, f32[64,32,2,48]{0,3,2,1:T(8,128)}, u32[]{:S(2)}) copy-start(f32[64,32,2,48]{0,3,2,1:T(8,128)} %copy-done.2) | copy-start | bytes 2359300
  178.8 4.0 %copy-start.24 = (s32[2]{0:T(128)S(1)}, s32[2]{0:T(128)}, u32[]{:S(2)}) copy-start(s32[2]{0:T(128)} %copy-done.23) | copy-start | bytes 28
  178.8 4.0 %copy-start.31 = (f32[2,8]{0,1:T(8,128)S(1)}, f32[2,8]{0,1:T(8,128)}, u32[]{:S(2)}) copy-start(f32[2,8]{0,1:T(8,128)} %get-tuple-element.7) | copy-start | bytes 196
  178.8 4.1 %copy-start.22 = (s32[2]{0:T(128)S(1)}, s32[2]{0:T(128)}, u32[]{:S(2)}) copy-start(s32[2]{0:T(128)} %copy-done.21) | copy-start | bytes 28
  178.8 4.1 %copy-start.33 = (f32[2,16]{1,0:T(2,128)S(1)}, f32[2,16]{1,0:T(2,128)}, u32[]{:S(2)}) copy-start(f32[2,16]{1,0:T(2,128)} %get-tuple-element.8) | copy-start | bytes 388
  178.8 4.3 %copy-start.9 = (f32[64,48]{0,1:T(8,128)S(1)}, f32[64,48]{0,1:T(8,128)}, u32[]{:S(2)}) copy-start(f32[64,48]{0,1:T(8,128)} %param.12) | copy-start | bytes 36868
  186.7 3.4 copy-start.11
  186.7 3.4 copy-start.15
  186.7 3.4 copy-start.29
  190.1 14.4 %copy-start.4 = (bf16[48,48,16,2]{1,2,3,0:T(8,128)(2,1)S(1)}, bf16[48,48,16,2]{1,2,3,0:T(8,128)(2,1)}, u32[]{:S(2)}) copy-start(bf16[48,48,16,2]{1,2,3,0:T(8,128)(2,1)} %get-tuple-element.18) | copy-start | bytes 442372
  191.4 93.5 %all-to-all-start.1 = ((bf16[2,64,128]{2,0,1:T(2,128)(2,1)}), bf16[2,64,128]{2,0,1:T(2,128)(2,1)S(1)}, u32[]{:S(2)}, u32[]{:S(2)}) async-start(bf16[2,64,128]{2,0,1:T(2,128)(2,1)} %reshape.198), calls=%async_computation.2 | async-start | bytes 65536 | tf_op jit(solution)/shard_map/all_to_all | solution.py:105
  204.6 97.0 %copy-start.13 = (s32[32]{0:T(128)S(1)}, s32[32]{0:T(128)}, u32[]{:S(2)}) copy-start(s32[32]{0:T(128)} %copy-done.12) | copy-start | bytes 388
  284.9 18.0 %all-to-all-start.2 = ((bf16[64,2,576]{2,1,0:T(2,128)(2,1)}), bf16[64,2,576]{2,1,0:T(2,128)(2,1)S(1)}, u32[]{:S(2)}, u32[]{:S(2)}) async-start(bf16[64,2,576]{2,1,0:T(2,128)(2,1)} %reshape.201), calls=%async_computation.3 | async-start | bytes 327680 | tf_op jit(solution)/shard_map/all_to_all | solution.py:120
  292.8 61.5 %all-reduce.4.cloned.1.call-start = ((), (), s32[]{:S(2)}) async-start(), calls=%async_computation.5 | async-start | bytes 327680
  302.9 4.9 %copy-start.20 = (f32[128,8]{0,1:T(8,128)S(1)}, f32[128,8]{0,1:T(8,128)}, u32[]{:S(2)}) copy-start(f32[128,8]{0,1:T(8,128)} %fusion.54) | copy-start | bytes 12292
  303.8 5.1 %copy-start.17 = (pred[16]{0:T(512)(128)(4,1)S(1)}, pred[16]{0:T(512)(128)(4,1)}, u32[]{:S(2)}) copy-start(pred[16]{0:T(512)(128)(4,1)} %copy-done.16) | copy-start | bytes 52
  303.8 5.1 %copy-start.19 = (s32[16]{0:T(128)S(1)}, s32[16]{0:T(128)}, u32[]{:S(2)}) copy-start(s32[16]{0:T(128)} %copy-done.18) | copy-start | bytes 196
  (7 other events, 11.9 us)
Sparse Core Ops, SparseCore 0:
  17.8 37.5 reduce-scatter.1
  309.0 45.1 all-reduce.3
where the time goes:
time: 370 us; the launch traced here: 363 us
  matrix products  98.8 us (27%)
  blocking collectives  86.1 us (23%)
  waiting for transfers between devices  76.7 us (21%)
  local copies, waits for them, and re-layouts  52.9 us (14%)
  starting transfers between devices  29.4 us (8%)
  between operations  15.9 us (4%)
    psum x1, blocking collectives, shards(): lax.psum((grad_in, grad_out, grad_x, grad_y, grad_z), ('px', 'py'))  77.6 us
    unnamed x3, waiting for transfers between devices  40.9 us
    dot_general x1, matrix products, shards(): grad_outer = jnp.dot(core_flow.T, core_matrix, precision=precise)  36.5 us
    reduce_scatter x1, waiting for transfers between devices, shards(): lax.psum_scatter(jnp.concatenate([term_in.reshape(ky_local * lax.axis_siz...  35.8 us
    reshape x1, local copies, waits for them, and re-layouts, shards(): core_matrix = tucker_core.reshape(RIN * ROUT * RX, RY * RZ)  15 us
    dot_general x3, matrix products, expand(): section = jnp.einsum('pqrn,ar->pqan', reshaped, fx, precision=precise)  14.8 us
    dot_general x1, local copies, waits for them, and re-layouts, shards(): grad_outer = jnp.dot(core_flow.T, core_matrix, precision=precise)  12.6 us
    all_to_all x1, starting transfers between devices, shards(): lax.all_to_all(x_synth, 'px', split_axis=1, concat_axis=0, tiled=True)  11.1 us
  transfers between devices with their start and end apart: 5, of which 2 were waited for; matrix products, arithmetic and copies ran while one was open for 11% of the time, Pallas kernels for 0%

commit v1 on v0

v1 whole, which is shorter than its diff:
```python
import math

import jax
import jax.numpy as jnp
import numpy as np
from jax import lax
from jax.experimental import pallas as pl
from jax.experimental.pallas import tpu as pltpu
from jax.sharding import PartitionSpec as P

NX = 128
NY = 128
NZ = 128
KX = 32
KY = 32
KZ = 16
RIN = 48
ROUT = 48
RX = 16
RY = 16
RZ = 8
C = 64

BF = jnp.bfloat16
F32 = jnp.float32
MESH = pl.DeviceIdType.MESH
EXACT = lax.Precision.HIGHEST
NN = (((1,), (0,)), ((), ()))
NT = (((1,), (1,)), ((), ()))
TN = (((0,), (0,)), ((), ()))


def table(count, length):
    half = count // 2
    rows = np.arange(count)[:, None]
    cols = np.arange(length)[None, :]
    freq = np.where(rows < half, rows, rows - half + 1)
    angle = (freq * cols % length) * (2.0 * math.pi / length)
    values = np.where(rows < half, np.cos(angle), np.sin(angle)) * math.sqrt(2.0 / length)
    return values.astype(np.float32)


def two_parts(values):
    high = values.astype(jnp.bfloat16)
    low = (values - high.astype(np.float32)).astype(jnp.bfloat16)
    return high, low


def constants():
    ex, ey, ez = table(KX, NX), table(KY, NY), table(KZ, NZ)
    eye8 = np.eye(8, dtype=np.float32)
    strips = ey.reshape(KY, 4, 32).transpose(1, 0, 2)
    fwd = np.einsum("pjy,cd->pjcdy", strips, eye8).reshape(4, 256, 256)
    bwd = np.ascontiguousarray(fwd.transpose(0, 2, 1))
    z_high, z_low = two_parts(ez)
    z_rows = np.concatenate([z_high, z_low], 0)
    z_block = np.einsum("kz,ij->ikjz", z_high.astype(np.float32), eye8).reshape(128, 1024)
    planes = ex.reshape(KX, 2, 8, 4, 2)
    eye2 = np.eye(2, dtype=np.float32)
    gather = np.einsum("ayzxp,mn->pmaznyx", planes, eye2).reshape(2, 64, 128)
    gather = np.concatenate(two_parts(gather), 1)
    spread = np.einsum("ayzxp,mn->znyxpma", planes, eye2).reshape(128, 128)
    spread = np.concatenate(two_parts(spread), 0)
    swap = np.zeros((8, 2, 8, 8, 16), np.float32)
    for z in range(8):
        for n in range(2):
            for m in range(8):
                swap[z, n, m, m, 2 * z + n] = 1.0
    swap = swap.reshape(128, 128)
    rows36 = np.zeros((8, 48, 2, 192), np.float32)
    for m in range(8):
        for i in range(36):
            rows36[m, i, m // 4, (m % 4) * 36 + i] = 1.0
    rows9 = np.zeros((4, 80, 8, 48), np.float32)
    for p in range(4):
        for q in range(9):
            for j in range(8):
                rows9[p, q * 8 + j, j, p * 9 + q] = 1.0
    widen = np.zeros((RX, RZ, RX, RY, RZ), np.float32)
    for r in range(RX):
        for t in range(RZ):
            widen[r, t, r, :, t] = 1.0
    mats = (
        fwd, bwd, z_rows, z_block, gather, spread, swap, np.ascontiguousarray(swap.T),
        rows36.reshape(384, 384), rows9.reshape(320, 384), widen.reshape(128, 2048),
    )
    return [np.asarray(m).astype(jnp.bfloat16) for m in mats]


X_CORE, X_YHI, X_A_YX, X_A_Z, X_D_Z, X_C_Z, X_E_Z, X_D_YX, X_C_YX, X_E_YX, X_D_PY, X_C_PY, X_E_PY, X_E_BACK = range(14)


def iota(shape, dim):
    return lax.broadcasted_iota(jnp.int32, shape, dim)


def flag(mask):
    return jnp.where(mask, 1.0, 0.0).astype(F32)


def dot(a, b, dims=NN, precision=None):
    return lax.dot_general(a, b, dims, precision=precision, preferred_element_type=F32)


def kernel(
    feat, cot, core, fin, fout, fx, fy, fz,
    k_fwd, k_bwd, k_zrows, k_zblock, k_gather, k_spread, k_swap, k_swapt, k_rows36, k_rows9, k_widen,
    out_features, out_core, out_small,
    field, core_v, fin_v, fout_v, fx_v, fy_v, fz_v,
    fwd, bwd, zrows, zblock, gather, spread, swap, swapt, rows36, rows9, widen,
    yspec, part, core_in, yhi_out, yhi_in, a_out, a_in, az_out, az_in,
    modes, uvt, uvp, d_out, d_in, w_all, c_out, c_in, e_out, e_in,
    dy_out, dy_in, cy_out, cy_in, ey_out, ey_in, dp_out, dp_in, cp_in, ep_out, ep_in, eb_out, eb_in,
    zspec,
    local_sem, send_sem, recv_sem,
):
    px = lax.axis_index("px")
    py = lax.axis_index("py")
    x4 = lax.rem(px, 4)
    z = lax.rem(px // 4, 8)
    y_lo = px // 32
    yx = y_lo * 4 + x4
    y_hi = py // 2
    half = lax.rem(py, 2)

    def at_z(other):
        return (y_lo * 32 + other * 4 + x4, py)

    def at_yx(other):
        return (other // 4 * 32 + z * 4 + lax.rem(other, 4), py)

    def at_py(other):
        return (px, other)

    loads = []

    def load(src, dst):
        copy = pltpu.make_async_copy(src, dst, local_sem.at[len(loads)])
        copy.start()
        loads.append(copy)
        return copy

    get_fwd = load(k_fwd.at[py], fwd)
    get_field = [[load(src.at[:, plane], field.at[plane, f]) for f, src in enumerate((feat, cot))] for plane in range(2)]
    get_zrows = load(k_zrows, zrows)
    get_small = [load(s, d) for s, d in ((fin, fin_v), (fout, fout_v), (fx, fx_v), (fy, fy_v), (fz, fz_v))]
    get_swap = load(k_swap, swap)
    get_gather = load(k_gather, gather)
    get_core = load(core, core_v)
    get_spread = load(k_spread, spread)
    get_rows36 = load(k_rows36, rows36)
    get_swapt = load(k_swapt, swapt)
    get_rows9 = load(k_rows9, rows9)
    get_bwd = load(k_bwd.at[py], bwd)
    get_zblock = load(k_zblock, zblock)
    get_widen = load(k_widen, widen)

    barrier = pltpu.get_barrier_semaphore()
    for d in range(1, 8):
        pl.semaphore_signal(barrier, inc=1, device_id=at_z(lax.rem(z + d, 8)), device_id_type=MESH)
        pl.semaphore_signal(barrier, inc=1, device_id=at_yx(lax.rem(yx + d, 8)), device_id_type=MESH)
    for d in range(1, 4):
        pl.semaphore_signal(barrier, inc=1, device_id=at_py(lax.rem(py + d, 4)), device_id_type=MESH)

    sends = []

    def send(number, slot_out, slot_in, src, dst, device):
        copy = pltpu.make_async_remote_copy(
            src_ref=src, dst_ref=dst, send_sem=send_sem.at[number, slot_out],
            recv_sem=recv_sem.at[number, slot_in], device_id=device, device_id_type=MESH,
        )
        copy.start()
        sends.append(copy)

    def receive(number, slot, dst):
        pltpu.make_async_remote_copy(
            src_ref=dst, dst_ref=dst, send_sem=send_sem.at[number, slot],
            recv_sem=recv_sem.at[number, slot], device_id=at_py(lax.rem(py + 1, 4)), device_id_type=MESH,
        ).wait_recv()

    def exchange(number, src_of, into, mine, size, device_of):
        for d in range(1, size):
            other = lax.rem(mine + d, size)
            send(number, d, mine, src_of(other), into.at[mine], device_of(other))
        into[mine] = src_of(mine)[...]

    def arrive(number, into, mine, size):
        for d in range(1, size):
            other = lax.rem(mine + d, size)
            receive(number, other, into.at[other])

    get_fwd.wait()
    for plane in range(2):
        for f in range(2):
            get_field[plane][f].wait()

            def lines(i, carry, plane=plane, f=f):
                pair = []
                for h in range(2):
                    block = field[plane, f, pl.ds(i * 16 + h * 8, 8)].reshape(256, NZ)
                    pair.append(dot(fwd[...], block).reshape(KY, 8, NZ))
                rows = pl.ds(pl.multiple_of(plane * 128 + f * 64 + i * 16, 16), 16)
                yspec[:, rows, :] = jnp.concatenate(pair, axis=1).astype(BF)
                return carry

            lax.fori_loop(0, 4, lines, 0, unroll=True)
    get_zrows.wait()

    def depth(group):
        def one(i, carry):
            both = dot(zrows[...], yspec[group * 8 + i], NT)
            part[group, i] = (both[:KZ] + both[KZ:]).astype(BF)
            return carry

        lax.fori_loop(0, 8, one, 0, unroll=4)

    for h in range(2):
        depth(h * 2 + (1 - half))
    pl.semaphore_wait(barrier, 17)
    for h in range(2):
        send(X_CORE, h, h, part.at[h * 2 + (1 - half)], core_in.at[h], at_py(y_hi * 2 + (1 - half)))
    for h in range(2):
        depth(h * 2 + half)

    far = 1 - y_hi
    for h in range(2):
        receive(X_CORE, h, core_in.at[h])
    yhi_out[...] = (part[far * 2 + half].astype(F32) + core_in[far].astype(F32)).astype(BF)
    send(X_YHI, 0, 0, yhi_out, yhi_in, at_py(far * 2 + half))
    near = part[y_hi * 2 + half].astype(F32) + core_in[y_hi].astype(F32)

    for copy in get_small:
        copy.wait()
    fin_t = dot(fin_v[...], flag(lax.rem(iota((C, 128), 1), C) == iota((C, 128), 0)), NN, EXACT)
    fout_t = fout_v[...]
    b_mode = py * 8 + yx
    y_rows = dot(flag(iota((64, KY), 1) == b_mode), fy_v[...], NT, EXACT)
    z_rows = dot(flag(iota((64, KZ), 1) == 2 * z + iota((64, KZ), 0) // 32), fz_v[...], NT, EXACT)
    y_wide = flag(iota((RY, 128), 1) // RZ == iota((RY, 128), 0))
    z_wide = flag(lax.rem(iota((RZ, 128), 1), RZ) == iota((RZ, 128), 0))
    y_lane = dot(y_rows, y_wide, NN, EXACT)
    z_lane = dot(z_rows, z_wide, NN, EXACT)
    yz_lane = y_lane * z_lane
    x_rep = dot(flag(iota((64, KX), 1) == lax.rem(iota((64, KX), 0), KX)), fx_v[...], NT, EXACT)
    for r in range(RX):
        modes[:, r * 128:(r + 1) * 128] = (x_rep[:, r:r + 1] * yz_lane).astype(BF)
    x_cols = dot(fx_v[...], flag(lax.rem(iota((KX, 64), 1), KX) == iota((KX, 64), 0)), NN, EXACT)
    x_cols = jnp.concatenate([x_cols, x_cols], axis=0)
    x_cols = jnp.where(iota((32, 64), 0) // RX == iota((32, 64), 1) // KX, x_cols, 0.0)
    x_high = x_cols.astype(BF)
    x_parts = jnp.concatenate([x_cols, x_cols - x_high.astype(F32)], axis=0).astype(BF)
    z_taps = dot(flag(iota((256, KZ), 0) // RX == iota((256, KZ), 1)), fz_v[...], NT, EXACT)
    z_taps = dot(z_taps, z_wide, NN, EXACT)
    z_taps = jnp.where(lax.rem(iota((256, 128), 0), RX) == iota((256, 128), 1) // RZ, z_taps, 0.0)
    z_high = z_taps.astype(BF)
    z_parts = jnp.concatenate([z_taps, z_taps - z_high.astype(F32)], axis=1).astype(BF)
    y_taps = dot(fy_v[...], y_wide, TN, EXACT)
    for block in range(8):
        for m in range(2):
            uvp[block, m * 192 + 144:(m + 1) * 192, :] = jnp.zeros((48, 64), BF)

    receive(X_YHI, 0, yhi_in)
    a_out[...] = (near + yhi_in[...].astype(F32)).astype(BF)

    exchange(X_A_YX, lambda o: a_out.at[o], a_in, yx, 8, at_yx)
    get_swap.wait()
    arrive(X_A_YX, a_in, yx, 8)
    az_out[...] = dot(swap[...], a_in[...].reshape(128, 256)).astype(BF).reshape(8, 16, 256)
    exchange(X_A_Z, lambda o: az_out.at[o], az_in, z, 8, at_z)
    get_gather.wait()
    arrive(X_A_Z, az_in, z, 8)
    slabs = az_in[...].reshape(128, 256)
    both = dot(gather[0], slabs[:, :128]) + dot(gather[1], slabs[:, 128:])
    spec = both[:64] + both[64:]
    spec_t = spec.T
    in_t, out_t = spec_t[:C], spec_t[C:]

    u_t = dot(fin_t[:, :C], in_t, NN, EXACT)
    v_t = dot(fout_t, out_t, NN, EXACT)
    for g in range(16):
        rows = u_t[g * 3:(g + 1) * 3][:, None, :] * v_t[None, :, :]
        rows = rows.reshape(144, 64)
        uvt[g * 144:(g + 1) * 144, :] = rows
        uvp[g % 8, (g // 8) * 192:(g // 8) * 192 + 144, :] = rows.astype(BF)
    for g in range(8):
        flow = dot(x_parts, uvp[g], NT)
        d_out[g] = (flow[:32] + flow[32:]).astype(BF)
    exchange(X_D_Z, lambda o: d_out.at[o], d_in, z, 8, at_z)

    get_core.wait()
    for g in range(8):
        w_all[g * 6:(g + 1) * 6] = dot(core_v[g * 288:(g + 1) * 288, :], modes[...], NT).reshape(6, 48, 64)
    weight = w_all[...]
    h_t = jnp.sum(weight * v_t[None, :, :], axis=1)
    pulled = dot(h_t, fin_t, TN, EXACT)
    lane = iota((64, 128), 1)
    pulled = jnp.concatenate(
        [jnp.where(lane < C, pulled, 0.0), jnp.where(lane >= C, pulled, 0.0)], axis=0
    ).astype(BF)
    get_spread.wait()
    synth = dot(spread[...], pulled)
    c_out[...] = (synth[:128] + synth[128:]).astype(BF).reshape(8, 16, 128)
    exchange(X_C_Z, lambda o: c_out.at[o], c_in, z, 8, at_z)

    g_t = jnp.sum(weight * u_t[:, None, :], axis=0)
    uv = uvt[...].T.astype(BF)
    acc = jnp.zeros((64, 128), F32)
    yz_sum = jnp.zeros((64, 128), F32)
    for g in range(8):
        flow = dot(uv, core_v[:, g * 256:(g + 1) * 256])
        for h in range(2):
            r = g * 2 + h
            piece = flow[:, h * 128:(h + 1) * 128]
            acc = acc + jnp.where(lane == 96 + r, jnp.sum(piece * yz_lane, axis=1, keepdims=True), 0.0)
            yz_sum = yz_sum + piece * x_rep[:, r:r + 1]
    row = iota((64, 128), 0)
    small = jnp.concatenate([acc[:32] + acc[32:], jnp.zeros((32, 128), F32)], axis=0)
    y_sum = jnp.sum(yz_sum * z_lane, axis=0, keepdims=True)
    z_sum = yz_sum * y_lane
    z_sum = [jnp.sum(z_sum[n * 32:(n + 1) * 32], axis=0, keepdims=True) for n in range(2)]
    sums = jnp.concatenate([y_sum, z_sum[0], z_sum[1], jnp.zeros((5, 128), F32)], axis=0)
    y_place = flag(iota((128, 128), 1) == 96 + iota((128, 128), 0) // RZ)
    z_place = flag(iota((128, 128), 1) == 112 + lax.rem(iota((128, 128), 0), RZ))
    y_put = dot(sums, y_place, NN, EXACT)
    z_put = dot(sums, z_place, NN, EXACT)
    small = small + jnp.where(row == 32 + b_mode, y_put[0:1], 0.0)
    small = small + jnp.where(row == 2 * z, z_put[1:2], 0.0) + jnp.where(row == 2 * z + 1, z_put[2:3], 0.0)
    h_pad = jnp.concatenate([h_t, jnp.zeros((80, 64), F32)], axis=0)
    g_pad = jnp.concatenate([jnp.zeros((48, 64), F32), g_t, jnp.zeros((32, 64), F32)], axis=0)
    small = small + dot(in_t, h_pad, NT, EXACT) + dot(out_t, g_pad, NT, EXACT)
    e_out[...] = small.reshape(8, 8, 128)
    exchange(X_E_Z, lambda o: e_out.at[o], e_in, z, 8, at_z)

    arrive(X_D_Z, d_in, z, 8)
    taps = dot(d_in[...].reshape(256, 384), z_parts, TN)
    taps = (taps[:, :128] + taps[:, 128:]).astype(BF)
    get_rows36.wait()
    dy_out[...] = dot(rows36[...], taps).astype(BF).reshape(8, 48, 128)
    exchange(X_D_YX, lambda o: dy_out.at[o], dy_in, yx, 8, at_yx)

    get_swapt.wait()
    arrive(X_C_Z, c_in, z, 8)
    cy_out[...] = dot(swapt[...], c_in[...].reshape(128, 128)).astype(BF).reshape(8, 16, 128)
    exchange(X_C_YX, lambda o: cy_out.at[o], cy_in, yx, 8, at_yx)

    arrive(X_E_Z, e_in, z, 8)
    ey_out[...] = jnp.sum(e_in[...], axis=0)
    exchange(X_E_YX, lambda o: ey_out, ey_in, yx, 8, at_yx)

    arrive(X_C_YX, cy_in, yx, 8)
    exchange(X_C_PY, lambda o: cy_in, cp_in, py, 4, at_py)
    get_rows9.wait()
    arrive(X_D_YX, dy_in, yx, 8)
    dp_out[...] = dot(rows9[...], dy_in[...].reshape(384, 128)).astype(BF).reshape(4, 80, 128)
    exchange(X_D_PY, lambda o: dp_out.at[o], dp_in, py, 4, at_py)
    arrive(X_E_YX, ey_in, yx, 8)
    ep_out[...] = jnp.sum(ey_in[...], axis=0)
    exchange(X_E_PY, lambda o: ep_out, ep_in, py, 4, at_py)

    get_bwd.wait()
    get_zblock.wait()
    arrive(X_C_PY, cp_in, py, 4)
    for g in range(4):
        deep = dot(cp_in[g].reshape(128, 128), zblock[...], TN)
        for i in range(4):
            pair = [deep[:, (2 * i + h) * 128:(2 * i + h + 1) * 128].reshape(16, 8, 128) for h in range(2)]
            zspec[:, g * 64 + i * 16:g * 64 + (i + 1) * 16, :] = jnp.concatenate(pair, axis=1).astype(BF)

    arrive(X_E_PY, ep_in, py, 4)
    eb_out[...] = jnp.sum(ep_in[...], axis=0)
    exchange(X_E_BACK, lambda o: eb_out, eb_in, z, 8, at_z)

    for plane in range(2):
        for i in range(8):
            lines = dot(bwd[...], zspec[plane * 8 + i])
            out_features[plane, i * 8:(i + 1) * 8] = lines.reshape(8, 32, 128).astype(BF)

    get_widen.wait()
    arrive(X_D_PY, dp_in, py, 4)
    rows = dp_in[...].reshape(320, 128)
    y_taps = y_taps.reshape(4, 1, 8, 128)
    for r in range(RX):
        wide = dot(rows, widen[:, r * 128:(r + 1) * 128]).reshape(4, 10, 8, 128) * y_taps
        out_core[:, r * 128:(r + 1) * 128] = jnp.sum(jnp.sum(wide, axis=0), axis=1)[:9]

    arrive(X_E_BACK, eb_in, z, 8)
    out_small[...] = eb_in[...].reshape(64, 128).T
    for copy in sends:
        copy.wait_send()


def write_out(planes, core_rows, small, features, core, g_in, g_out, g_x, g_y, g_z, x_v, y_v, z_v, sem):
    copies = [pltpu.make_async_copy(planes.at[i], features.at[:, i], sem.at[i]) for i in range(2)]
    copies.append(pltpu.make_async_copy(core_rows, core, sem.at[2]))
    copies.append(pltpu.make_async_copy(small.at[0:48], g_in, sem.at[3]))
    copies.append(pltpu.make_async_copy(small.at[48:96], g_out, sem.at[4]))
    for copy in copies:
        copy.start()
    x_v[...] = small[96:112, 0:32]
    y_v[...] = small[96:112, 32:64]
    z_v[...] = small[112:120, 0:16]
    for i, (src, dst) in enumerate(((x_v, g_x), (y_v, g_y), (z_v, g_z))):
        copies.append(pltpu.make_async_copy(src, dst, sem.at[5 + i]))
        copies[-1].start()
    for copy in copies:
        copy.wait()


def shards(features, cotangent, tucker_core, in_factor, out_factor, x_factor, y_factor, z_factor):
    tables = [jnp.asarray(m) for m in constants()]
    hbm = pl.BlockSpec(memory_space=pltpu.HBM)
    vmem = pl.BlockSpec(memory_space=pltpu.VMEM)
    buffers = [
        ((2, 2, 64, 32, 128), BF), ((2304, 2048), BF), ((48, 64), F32), ((48, 64), F32), ((16, 32), F32),
        ((16, 32), F32), ((8, 16), F32),
        ((256, 256), BF), ((256, 256), BF), ((32, 128), BF), ((128, 1024), BF), ((2, 128, 128), BF),
        ((256, 128), BF), ((128, 128), BF), ((128, 128), BF), ((384, 384), BF), ((320, 384), BF), ((128, 2048), BF),
        ((32, 256, 128), BF), ((4, 8, 16, 256), BF), ((2, 8, 16, 256), BF), ((8, 16, 256), BF), ((8, 16, 256), BF),
        ((8, 16, 256), BF), ((8, 16, 256), BF), ((8, 16, 256), BF), ((8, 16, 256), BF),
        ((64, 2048), BF), ((2304, 64), F32), ((8, 384, 64), BF), ((8, 32, 384), BF), ((8, 32, 384), BF),
        ((48, 48, 64), F32), ((8, 16, 128), BF), ((8, 16, 128), BF), ((8, 8, 128), F32), ((8, 8, 128), F32),
        ((8, 48, 128), BF), ((8, 48, 128), BF), ((8, 16, 128), BF), ((8, 16, 128), BF),
        ((8, 128), F32), ((8, 8, 128), F32), ((4, 80, 128), BF), ((4, 80, 128), BF), ((4, 8, 16, 128), BF),
        ((8, 128), F32), ((4, 8, 128), F32), ((8, 128), F32), ((8, 8, 128), F32),
        ((16, 256, 128), BF),
    ]
    factors = (in_factor, out_factor, x_factor, y_factor, z_factor)
    operands = [features, cotangent, tucker_core] + [a.T for a in factors] + tables
    planes, core_rows, small = pl.pallas_call(
        kernel,
        out_shape=(
            jax.ShapeDtypeStruct((2, C, 32, NZ), BF),
            jax.ShapeDtypeStruct((9, 2048), F32),
            jax.ShapeDtypeStruct((128, 64), F32),
        ),
        in_specs=[hbm] * (8 + len(tables)),
        out_specs=(vmem, vmem, vmem),
        scratch_shapes=[pltpu.VMEM(shape, dtype) for shape, dtype in buffers] + [
            pltpu.SemaphoreType.DMA((24,)),
            pltpu.SemaphoreType.DMA((14, 8)),
            pltpu.SemaphoreType.DMA((14, 8)),
        ],
        compiler_params=pltpu.CompilerParams(
            collective_id=0, has_side_effects=True, vmem_limit_bytes=32 * 1024 * 1024
        ),
    )(*[pltpu.with_memory_space_constraint(a, pltpu.HBM) for a in operands])
    outs = pl.pallas_call(
        write_out,
        out_shape=(
            jax.ShapeDtypeStruct((C, 2, 32, NZ), BF),
            jax.ShapeDtypeStruct((9, 2048), F32),
            jax.ShapeDtypeStruct((RIN, C), F32),
            jax.ShapeDtypeStruct((ROUT, C), F32),
            jax.ShapeDtypeStruct((RX, KX), F32),
            jax.ShapeDtypeStruct((RY, KY), F32),
            jax.ShapeDtypeStruct((RZ, KZ), F32),
        ),
        in_specs=[vmem] * 3,
        out_specs=[hbm] * 7,
        scratch_shapes=[
            pltpu.VMEM((RX, KX), F32), pltpu.VMEM((RY, KY), F32), pltpu.VMEM((RZ, KZ), F32),
            pltpu.SemaphoreType.DMA((8,)),
        ],
    )(planes, core_rows, small)
    return outs[0], outs[1], outs[2].T, outs[3].T, outs[4].T, outs[5].T, outs[6].T


def solution(mesh):
    placed = (P(None, "px", "py", None), P(None, "px", "py", None), P(), P(), P(), P(), P(), P())
    return jax.shard_map(
        shards,
        mesh=mesh,
        in_specs=placed,
        out_specs=(P(None, "px", "py", None), P(("px", "py"), None), P(), P(), P(), P(), P()),
        check_vma=False,
    )
```

time: 370 us -> 55 us (0.15); the launches traced: 363 us -> 54.9 us
  matrix products: 98.8 us -> 0 us
  blocking collectives: 86.1 us -> 0 us
  waiting for transfers between devices: 76.7 us -> 0 us
  Pallas kernels: 0 us -> 52 us
  local copies, waits for them, and re-layouts: 52.9 us -> 2.23 us
  starting transfers between devices: 29.4 us -> 0 us
  between operations: 15.9 us -> 0.65 us
    dot_general x27 -> x0, matrix products: 98.8 us -> none  [the longest x1 36.5 us: shards(): grad_outer = jnp.dot(core_flow.T, core_matrix, precision=precise)]
    psum x1 -> x0, blocking collectives: 77.6 us -> none  [shards(): lax.psum((grad_in, grad_out, grad_x, grad_y, grad_z), ('px', 'py'))]
    pallas_call x0 -> x2, Pallas kernels: none -> 52 us  [the longest x1 49.6 us: shards(): pl.pallas_call(kernel, out_shape=(jax.ShapeDtypeStruct((2, C, 32, NZ), BF...]
    unnamed x3 -> x0, waiting for transfers between devices: 40.9 us -> none
    reduce_scatter x1 -> x0, waiting for transfers between devices: 35.8 us -> none  [shards(): lax.psum_scatter(jnp.concatenate([term_in.reshape(ky_local * lax.axis_siz...]
    all_to_all x3 -> x0, starting transfers between devices: 29.3 us -> none  [the longest x1 11.1 us: shards(): lax.all_to_all(x_synth, 'px', split_axis=1, concat_axis=0, tiled=True)]
    reshape x8 -> x0, local copies, waits for them, and re-layouts: 20.5 us -> none  [the longest x1 15 us: shards(): core_matrix = tucker_core.reshape(RIN * ROUT * RX, RY * RZ)]
    dot_general x1 -> x0, local copies, waits for them, and re-layouts: 12.6 us -> none  [shards(): grad_outer = jnp.dot(core_flow.T, core_matrix, precision=precise)]
  transfers between devices with their start and end apart: 5 -> 0, of which waited for: 2 -> 0; matrix products, arithmetic and copies ran while one was open for 11% -> 0% of each run, Pallas kernels for 0% -> 0%
where the time goes in v1:
time: 55 us; the launch traced here: 54.9 us
  Pallas kernels  52 us (95%)
  local copies, waits for them, and re-layouts  2.23 us (4%)
  between operations  0.65 us (1%)
    pallas_call x1, Pallas kernels, shards(): pl.pallas_call(kernel, out_shape=(jax.ShapeDtypeStruct((2, C, 32, NZ), BF...  49.6 us
    pallas_call x1, Pallas kernels, shards(): pl.pallas_call(write_out, out_shape=(jax.ShapeDtypeStruct((C, 2, 32, NZ),...  2.38 us
    unnamed x6, local copies, waits for them, and re-layouts  2.23 us

profile of v1, /device:TPU:1, one launch (start us, length us, event | category | flops | bytes accessed | tf_op | source)
XLA Modules:
  0.0 54.9 jit_solution(11367524501159230424)
XLA Ops:
  0.6 49.6 %shard_map.234 = (bf16[2,64,32,128]{3,2,1,0:T(8,128)(2,1)S(1)}, f32[9,2048]{1,0:T(8,128)S(1)}, f32[128,64]{1,0:T(8,128)S(1)}) custom-call(bf16[64,2,32,128]{3,2,1,0:T(8,128)(2,1)} %feat.1, bf16[64,2,32,128]{3,2,1,0:T(8,128)(2,1)} %cot.1, bf16[2304,2048]{1,0:T(8,128)(2,1)} %core.1, f32[48,64]{1,0:T(8,128)} %bitcast.10, f32[48,64]{1,0:T(8,128)} %bitcast.11, ...), custom_call_target="tpu_custom_call" | custom-call | tf_op jit(solution)/shard_map/pallas_call | solution.py:429
  50.2 0.0 copy-start
  50.2 1.0 %copy-done = bf16[2,64,32,128]{3,2,1,0:T(8,128)(2,1)} copy-done((bf16[2,64,32,128]{3,2,1,0:T(8,128)(2,1)}, bf16[2,64,32,128]{3,2,1,0:T(8,128)(2,1)S(1)}, u32[]{:S(2)}) %copy-start) | copy-done | bytes 1048600
  51.2 0.0 copy-start.1
  51.2 0.6 %copy-done.1 = f32[9,2048]{1,0:T(8,128)} copy-done((f32[9,2048]{1,0:T(8,128)}, f32[9,2048]{1,0:T(8,128)S(1)}, u32[]{:S(2)}) %copy-start.1) | copy-done | bytes 73752
  51.8 0.0 copy-start.2
  51.8 0.6 %copy-done.2 = f32[128,64]{1,0:T(8,128)} copy-done((f32[128,64]{1,0:T(8,128)}, f32[128,64]{1,0:T(8,128)S(1)}, u32[]{:S(2)}) %copy-start.2) | copy-done | bytes 32792
  52.5 2.4 %shard_map.235 = (bf16[64,2,32,128]{3,2,1,0:T(8,128)(2,1)}, f32[9,2048]{1,0:T(8,128)}, f32[48,64]{1,0:T(8,128)}, f32[48,64]{1,0:T(8,128)}, f32[16,32]{1,0:T(8,128)}, /*index=5*/f32[16,32]{1,0:T(8,128)}, f32[8,16]{1,0:T(8,128)}) custom-call(bf16[2,64,32,128]{3,2,1,0:T(8,128)(2,1)} %copy-done, f32[9,2048]{1,0:T(8,128)} %copy-done.1, f32[128,64]{1,0:T(8,128)} %copy-done.2), custom_call_target="tpu_custom_call" | custom-call | tf_op jit(solution)/shard_map/pallas_call | solution.py:447
Async XLA Ops:
  50.2 1.0 %copy-start = (bf16[2,64,32,128]{3,2,1,0:T(8,128)(2,1)}, bf16[2,64,32,128]{3,2,1,0:T(8,128)(2,1)S(1)}, u32[]{:S(2)}) copy-start(bf16[2,64,32,128]{3,2,1,0:T(8,128)(2,1)S(1)} %get-tuple-element.17.planes) | copy-start | bytes 3145732
  51.2 0.6 %copy-start.1 = (f32[9,2048]{1,0:T(8,128)}, f32[9,2048]{1,0:T(8,128)S(1)}, u32[]{:S(2)}) copy-start(f32[9,2048]{1,0:T(8,128)S(1)} %get-tuple-element.18.core_rows) | copy-start | bytes 221188
  51.8 0.6 %copy-start.2 = (f32[128,64]{1,0:T(8,128)}, f32[128,64]{1,0:T(8,128)S(1)}, u32[]{:S(2)}) copy-start(f32[128,64]{1,0:T(8,128)S(1)} %get-tuple-element.19.small) | copy-start | bytes 98308

commit v2 on v1

v2 whole, which is shorter than its diff:
```python
import math

import jax
import jax.numpy as jnp
import numpy as np
from jax import lax
from jax.experimental import pallas as pl
from jax.experimental.pallas import tpu as pltpu
from jax.sharding import PartitionSpec as P

NX = 128
NY = 128
NZ = 128
KX = 32
KY = 32
KZ = 16
RIN = 48
ROUT = 48
RX = 16
RY = 16
RZ = 8
C = 64

BF = jnp.bfloat16
F32 = jnp.float32
MESH = pl.DeviceIdType.MESH
EXACT = lax.Precision.HIGHEST
NN = (((1,), (0,)), ((), ()))
NT = (((1,), (1,)), ((), ()))
TN = (((0,), (0,)), ((), ()))


def table(count, length):
    half = count // 2
    rows = np.arange(count)[:, None]
    cols = np.arange(length)[None, :]
    freq = np.where(rows < half, rows, rows - half + 1)
    angle = (freq * cols % length) * (2.0 * math.pi / length)
    values = np.where(rows < half, np.cos(angle), np.sin(angle)) * math.sqrt(2.0 / length)
    return values.astype(np.float32)


def two_parts(values):
    high = values.astype(jnp.bfloat16)
    low = (values - high.astype(np.float32)).astype(jnp.bfloat16)
    return high, low


def constants():
    ex, ey, ez = table(KX, NX), table(KY, NY), table(KZ, NZ)
    eye8 = np.eye(8, dtype=np.float32)
    strips = ey.reshape(KY, 4, 32).transpose(1, 0, 2)
    fwd = np.einsum("pjy,cd->pjcdy", strips, eye8).reshape(4, 256, 256)
    bwd = np.ascontiguousarray(fwd.transpose(0, 2, 1))
    z_high, z_low = two_parts(ez)
    z_rows = np.concatenate([z_high, z_low], 0)
    z_block = np.einsum("kz,ij->ikjz", z_high.astype(np.float32), eye8).reshape(128, 1024)
    planes = ex.reshape(KX, 2, 8, 4, 2)
    eye2 = np.eye(2, dtype=np.float32)
    gather = np.einsum("ayzxp,mn->pmaznyx", planes, eye2).reshape(2, 64, 128)
    gather = np.concatenate(two_parts(gather), 1)
    spread = np.einsum("ayzxp,mn->znyxpma", planes, eye2).reshape(128, 128)
    spread = np.concatenate(two_parts(spread), 0)
    swap = np.zeros((8, 2, 8, 8, 16), np.float32)
    for z in range(8):
        for n in range(2):
            for m in range(8):
                swap[z, n, m, m, 2 * z + n] = 1.0
    swap = swap.reshape(128, 128)
    swap_add = np.concatenate([swap, swap], 1)
    rows9 = np.zeros((2, 8, 2, 16, 2, 192), np.float32)
    for h in range(2):
        for m in range(8):
            for c in range(2):
                for q in range(9):
                    rows9[h, m, c, q, m // 4, (m % 4) * 36 + (h * 2 + c) * 9 + q] = 1.0
    widen = np.zeros((RX, RZ, RX, RY, RZ), np.float32)
    for r in range(RX):
        for t in range(RZ):
            widen[r, t, r, :, t] = 1.0
    mats = (
        fwd, bwd, z_rows, z_block, gather, spread, swap_add, np.ascontiguousarray(swap.T),
        rows9.reshape(512, 384), widen.reshape(128, 2048),
    )
    return [np.asarray(m).astype(jnp.bfloat16) for m in mats]


(
    X_A_CORE, X_A_XY, X_A_Z, X_D_Z, X_C_Z, X_D_XY, X_C_XY, X_D_CORE, X_C_CORE,
    X_G_SPLIT, X_G_Z, X_G_X, X_G_Y, X_G_CORE, X_F_Z, X_F_X, X_F_Y, X_F_CORE,
) = range(18)


def iota(shape, dim):
    return lax.broadcasted_iota(jnp.int32, shape, dim)


def flag(mask):
    return jnp.where(mask, 1.0, 0.0).astype(F32)


def dot(a, b, dims=NN, precision=None):
    return lax.dot_general(a, b, dims, precision=precision, preferred_element_type=F32)


def kernel(
    feat, cot, core, fin, fout, fx, fy, fz,
    k_fwd, k_bwd, k_zrows, k_zblock, k_gather, k_spread, k_swap, k_swapt, k_rows9, k_widen,
    out_features, out_core, out_pair, out_modes,
    field, core_v, fin_v, fout_v, fx_v, fy_v, fz_v,
    fwd, bwd, zrows, zblock, gather, spread, swap, swapt, rows9, widen,
    yspec, part, core_in, a_out, a_in, az_out, az_in,
    modes, uvt, uvp, d_out, d_in, w_all, c_out, c_in,
    g_out, gs_in, gz_out, gz_in, gx_out, gx_in, gy_out, gy_in, gc_out, gc_in,
    f_out, fz_in, fx_out, fx_in, fy_out, fy_in, fc_out, fc_in,
    dy_out, dy_in, dc_in, cy_out, cp_in,
    zspec, local_sem, send_sem, recv_sem,
):
    px = lax.axis_index("px")
    py = lax.axis_index("py")
    x4 = lax.rem(px, 4)
    z = lax.rem(px // 4, 8)
    y_lo = px // 32
    yx = y_lo * 4 + x4
    y_hi = py // 2
    half = lax.rem(py, 2)
    y = y_hi * 2 + y_lo
    xy = y * 4 + x4
    other_core = (px, y_hi * 2 + 1 - half)

    def at_z(other):
        return (y_lo * 32 + other * 4 + x4, py)

    def at_xy(other):
        there = lax.rem(other, 8)
        return (there // 4 * 32 + z * 4 + lax.rem(there, 4), other // 8 * 2 + half)

    def at_x(other):
        return (y_lo * 32 + z * 4 + other, py)

    def at_y(other):
        return (lax.rem(other, 2) * 32 + z * 4 + x4, other // 2 * 2 + half)

    along_z = [lax.rem(z + d, 8) for d in (4, 3, 5, 2, 6, 1, 7)]
    along_x = [lax.rem(x4 + d, 4) for d in (2, 1, 3)]
    along_y = [lax.rem(y + d, 4) for d in (2, 1, 3)]
    along_xy = [
        lax.rem(y + dy, 4) * 4 + lax.rem(x4 + dx, 4)
        for dy, dx in (
            (2, 2), (2, 1), (2, 3), (1, 2), (3, 2), (2, 0), (0, 2), (1, 1),
            (1, 3), (3, 1), (3, 3), (1, 0), (3, 0), (0, 1), (0, 3),
        )
    ]

    loads = []

    def load(src, dst):
        copy = pltpu.make_async_copy(src, dst, local_sem.at[len(loads)])
        copy.start()
        loads.append(copy)
        return copy

    get_fwd = load(k_fwd.at[py], fwd)
    get_field = [
        [load(src.at[i * 16:(i + 1) * 16], field.at[f, i * 16:(i + 1) * 16]) for f, src in enumerate((feat, cot))]
        for i in range(4)
    ]

    barrier = pltpu.get_barrier_semaphore()
    for other in along_z:
        pl.semaphore_signal(barrier, inc=1, device_id=at_z(other), device_id_type=MESH)
    for other in along_xy:
        pl.semaphore_signal(barrier, inc=1, device_id=at_xy(other), device_id_type=MESH)
    pl.semaphore_signal(barrier, inc=1, device_id=other_core, device_id_type=MESH)

    get_zrows = load(k_zrows, zrows)
    get_small = [load(s, d) for s, d in ((fin, fin_v), (fout, fout_v), (fx, fx_v), (fy, fy_v), (fz, fz_v))]
    get_swap = load(k_swap, swap)
    get_gather = load(k_gather, gather)
    get_core = load(core, core_v)
    get_spread = load(k_spread, spread)
    get_rows9 = load(k_rows9, rows9)
    get_swapt = load(k_swapt, swapt)
    get_zblock = load(k_zblock, zblock)
    get_bwd = load(k_bwd.at[py], bwd)
    get_widen = load(k_widen, widen)

    sends = []

    def send(number, slot_out, slot_in, src, dst, device):
        copy = pltpu.make_async_remote_copy(
            src_ref=src, dst_ref=dst, send_sem=send_sem.at[number, slot_out],
            recv_sem=recv_sem.at[number, slot_in], device_id=device, device_id_type=MESH,
        )
        copy.start()
        sends.append(copy)

    def receive(number, slot, dst):
        pltpu.make_async_remote_copy(
            src_ref=dst, dst_ref=dst, send_sem=send_sem.at[number, slot],
            recv_sem=recv_sem.at[number, slot], device_id=other_core, device_id_type=MESH,
        ).wait_recv()

    def exchange(number, src_of, into, mine, others, device_of):
        for d, other in enumerate(others):
            send(number, d, mine, src_of(other), into.at[mine], device_of(other))
        into[mine] = src_of(mine)[...]

    def arrive(number, into, others):
        for other in others[::-1]:
            receive(number, other, into.at[other])

    get_fwd.wait()
    for i in range(4):
        for f in range(2):
            get_field[i][f].wait()

            def lines(plane, carry, i=i, f=f):
                pair = []
                for h in range(2):
                    c = i * 16 + h * 8
                    block = field[f, c:c + 8, plane].reshape(256, NZ)
                    pair.append(dot(fwd[...], block).reshape(KY, 8, NZ))
                rows = pl.ds(pl.multiple_of(plane * 128 + f * 64 + i * 16, 16), 16)
                yspec[:, rows, :] = jnp.concatenate(pair, axis=1).astype(BF)
                return carry

            lax.fori_loop(0, 2, lines, 0, unroll=True)
    get_zrows.wait()

    def depth(group):
        def one(i, carry):
            both = dot(zrows[...], yspec[group * 8 + i], NT)
            part[group, i] = (both[:KZ] + both[KZ:]).astype(BF)
            return carry

        lax.fori_loop(0, 8, one, 0, unroll=4)

    for h in range(2):
        depth(h * 2 + (1 - half))
    pl.semaphore_wait(barrier, 23)
    for h in range(2):
        send(X_A_CORE, h, h, part.at[h * 2 + (1 - half)], core_in.at[h], other_core)
    for h in range(2):
        depth(h * 2 + half)

    for h in range(2):
        receive(X_A_CORE, h, core_in.at[h])
        a_out[h * 8:(h + 1) * 8] = (part[h * 2 + half].astype(F32) + core_in[h].astype(F32)).astype(BF)
    exchange(X_A_XY, lambda o: a_out.at[o], a_in, xy, along_xy, at_xy)

    for copy in get_small:
        copy.wait()
    fin_t = dot(fin_v[...], flag(lax.rem(iota((C, 128), 1), C) == iota((C, 128), 0)), NN, EXACT)
    fout_t = fout_v[...]
    b_mode = py * 8 + yx
    y_rows = dot(flag(iota((64, KY), 1) == b_mode), fy_v[...], NT, EXACT)
    z_rows = dot(flag(iota((64, KZ), 1) == 2 * z + iota((64, KZ), 0) // 32), fz_v[...], NT, EXACT)
    y_wide = flag(iota((RY, 128), 1) // RZ == iota((RY, 128), 0))
    z_wide = flag(lax.rem(iota((RZ, 128), 1), RZ) == iota((RZ, 128), 0))
    y_lane = dot(y_rows, y_wide, NN, EXACT)
    z_lane = dot(z_rows, z_wide, NN, EXACT)
    yz_lane = y_lane * z_lane
    x_rep = dot(flag(iota((64, KX), 1) == lax.rem(iota((64, KX), 0), KX)), fx_v[...], NT, EXACT)
    for r in range(RX):
        modes[:, r * 128:(r + 1) * 128] = (x_rep[:, r:r + 1] * yz_lane).astype(BF)
    x_cols = dot(fx_v[...], flag(lax.rem(iota((KX, 64), 1), KX) == iota((KX, 64), 0)), NN, EXACT)
    x_cols = jnp.concatenate([x_cols, x_cols], axis=0)
    x_cols = jnp.where(iota((32, 64), 0) // RX == iota((32, 64), 1) // KX, x_cols, 0.0)
    x_high = x_cols.astype(BF)
    x_parts = jnp.concatenate([x_cols, x_cols - x_high.astype(F32)], axis=0).astype(BF)
    z_taps = dot(flag(iota((256, KZ), 0) // RX == iota((256, KZ), 1)), fz_v[...], NT, EXACT)
    z_taps = dot(z_taps, z_wide, NN, EXACT)
    z_taps = jnp.where(lax.rem(iota((256, 128), 0), RX) == iota((256, 128), 1) // RZ, z_taps, 0.0)
    z_high = z_taps.astype(BF)
    z_parts = jnp.concatenate([z_taps, z_taps - z_high.astype(F32)], axis=1).astype(BF)
    y_taps = dot(fy_v[...], y_wide, TN, EXACT)
    for block in range(8):
        for m in range(2):
            uvp[block, m * 192 + 144:(m + 1) * 192, :] = jnp.zeros((48, 64), BF)

    get_swap.wait()
    arrive(X_A_XY, a_in, along_xy)
    az_out[...] = dot(swap[...], a_in[...].reshape(256, 256)).astype(BF).reshape(8, 16, 256)
    exchange(X_A_Z, lambda o: az_out.at[o], az_in, z, along_z, at_z)

    get_core.wait()
    for g in range(8):
        w_all[g * 6:(g + 1) * 6] = dot(core_v[g * 288:(g + 1) * 288, :], modes[...], NT).reshape(6, 48, 64)

    get_gather.wait()
    arrive(X_A_Z, az_in, along_z)
    slabs = az_in[...].reshape(128, 256)
    both = dot(gather[0], slabs[:, :128]) + dot(gather[1], slabs[:, 128:])
    spec = both[:64] + both[64:]
    spec_t = spec.T

    u_t = dot(fin_t[:, :C], spec_t[:C], NN, EXACT)
    v_t = dot(fout_t, spec_t[C:], NN, EXACT)
    for g in range(16):
        rows = u_t[g * 3:(g + 1) * 3][:, None, :] * v_t[None, :, :]
        rows = rows.reshape(144, 64)
        uvt[g * 144:(g + 1) * 144, :] = rows
        uvp[g % 8, (g // 8) * 192:(g // 8) * 192 + 144, :] = rows.astype(BF)
    for g in range(8):
        flow = dot(x_parts, uvp[g], NT)
        d_out[g] = (flow[:32] + flow[32:]).astype(BF)
    exchange(X_D_Z, lambda o: d_out.at[o], d_in, z, along_z, at_z)

    weight = w_all[...]
    h_t = jnp.sum(weight * v_t[None, :, :], axis=1)
    pulled = dot(h_t, fin_t, TN, EXACT)
    lane = iota((64, 128), 1)
    pulled = jnp.concatenate(
        [jnp.where(lane < C, pulled, 0.0), jnp.where(lane >= C, pulled, 0.0)], axis=0
    ).astype(BF)
    get_spread.wait()
    synth = dot(spread[...], pulled)
    c_out[...] = (synth[:128] + synth[128:]).astype(BF).reshape(8, 16, 128)
    exchange(X_C_Z, lambda o: c_out.at[o], c_in, z, along_z, at_z)

    g_t = jnp.sum(weight * u_t[:, None, :], axis=0)
    for f, ranks in enumerate((h_t, g_t)):
        grad = dot(ranks, spec[:, f * C:(f + 1) * C], NN, EXACT)
        g_out[f] = jnp.concatenate([grad[:24], grad[24:]], axis=1)
    send(X_G_SPLIT, 0, 0, g_out.at[1 - half], gs_in, other_core)

    uv = uvt[...].T.astype(BF)
    x_sum = jnp.zeros((64, 128), F32)
    yz_sum = jnp.zeros((64, 128), F32)
    for g in range(8):
        flow = dot(uv, core_v[:, g * 256:(g + 1) * 256])
        for h in range(2):
            r = g * 2 + h
            piece = flow[:, h * 128:(h + 1) * 128]
            x_sum = x_sum + jnp.where(lane == r, jnp.sum(piece * yz_lane, axis=1, keepdims=True), 0.0)
            yz_sum = yz_sum + piece * x_rep[:, r:r + 1]
    row16 = iota((16, 128), 0)
    lane16 = iota((16, 128), 1)
    modes_grad = dot(
        flag(iota((16, 128), 0) == iota((16, 128), 1)), x_sum[:32] + x_sum[32:], NT, EXACT
    )
    modes_grad = jnp.concatenate([modes_grad, jnp.zeros((16, 96), F32)], axis=1)
    y_sum = jnp.sum(yz_sum * z_lane, axis=0, keepdims=True)
    y_pick = flag(iota((16, 128), 1) // RZ == row16)
    y_col = jnp.sum(y_pick * y_sum, axis=1, keepdims=True)
    modes_grad = modes_grad + jnp.where(lane16 == 32 + b_mode, y_col, 0.0)
    z_pick = flag(lax.rem(iota((16, 128), 1), RZ) == row16)
    z_sum = yz_sum * y_lane
    for n in range(2):
        z_col = jnp.sum(z_pick * jnp.sum(z_sum[n * 32:(n + 1) * 32], axis=0, keepdims=True), axis=1, keepdims=True)
        modes_grad = modes_grad + jnp.where(lane16 == 64 + 2 * z + n, z_col, 0.0)
    f_out[...] = modes_grad
    exchange(X_F_Z, lambda o: f_out, fz_in, z, along_z, at_z)

    receive(X_G_SPLIT, 0, gs_in)
    gz_out[...] = g_out[half] + gs_in[...]
    exchange(X_G_Z, lambda o: gz_out, gz_in, z, along_z, at_z)

    arrive(X_D_Z, d_in, along_z)
    taps = dot(d_in[...].reshape(256, 384), z_parts, TN)
    taps = (taps[:, :128] + taps[:, 128:]).astype(BF)
    get_rows9.wait()
    dy_out[...] = dot(rows9[...], taps).astype(BF).reshape(16, 32, 128)
    exchange(X_D_XY, lambda o: dy_out.at[o], dy_in, xy, along_xy, at_xy)

    get_swapt.wait()
    arrive(X_C_Z, c_in, along_z)
    cy_out[...] = dot(swapt[...], c_in[...].reshape(128, 128)).astype(BF).reshape(8, 16, 128)
    exchange(X_C_XY, lambda o: cy_out.at[lax.rem(o, 8)], cp_in.at[half], xy, along_xy, at_xy)

    arrive(X_F_Z, fz_in, along_z)
    fx_out[...] = jnp.sum(fz_in[...], axis=0)
    exchange(X_F_X, lambda o: fx_out, fx_in, x4, along_x, at_x)
    arrive(X_G_Z, gz_in, along_z)
    gx_out[...] = jnp.sum(gz_in[...], axis=0)
    exchange(X_G_X, lambda o: gx_out, gx_in, x4, along_x, at_x)
    arrive(X_F_X, fx_in, along_x)
    fy_out[...] = jnp.sum(fx_in[...], axis=0)
    exchange(X_F_Y, lambda o: fy_out, fy_in, y, along_y, at_y)
    arrive(X_G_X, gx_in, along_x)
    gy_out[...] = jnp.sum(gx_in[...], axis=0)
    exchange(X_G_Y, lambda o: gy_out, gy_in, y, along_y, at_y)

    arrive(X_C_XY, cp_in.at[half], along_xy)
    send(X_C_CORE, 0, 0, cp_in.at[half], cp_in.at[half], other_core)
    arrive(X_D_XY, dy_in, along_xy)
    theirs = pl.ds(pl.multiple_of((1 - half) * 16, 16), 16)
    ours = pl.ds(pl.multiple_of(half * 16, 16), 16)
    send(X_D_CORE, 0, 0, dy_in.at[:, theirs], dc_in, other_core)

    def deepen(group, modes_of):
        deep = dot(modes_of.reshape(128, 128), zblock[...], TN)
        for i in range(4):
            pair = [deep[:, (2 * i + h) * 128:(2 * i + h + 1) * 128].reshape(16, 8, 128) for h in range(2)]
            rows = pl.ds(pl.multiple_of(group * 64 + i * 16, 16), 16)
            zspec[:, rows, :] = jnp.concatenate(pair, axis=1).astype(BF)

    get_zblock.wait()
    for h in range(2):
        deepen(h * 2 + half, cp_in[half, h * 8:(h + 1) * 8])
    arrive(X_F_Y, fy_in, along_y)
    fc_out[...] = jnp.sum(fy_in[...], axis=0)
    send(X_F_CORE, 0, 0, fc_out, fc_in, other_core)
    arrive(X_G_Y, gy_in, along_y)
    gc_out[...] = jnp.sum(gy_in[...], axis=0)
    send(X_G_CORE, 0, 0, gc_out, gc_in, other_core)
    receive(X_C_CORE, 0, cp_in.at[1 - half])
    for h in range(2):
        deepen(h * 2 + 1 - half, cp_in[1 - half, h * 8:(h + 1) * 8])
    get_bwd.wait()
    for plane in range(2):
        for i in range(8):
            lines = dot(bwd[...], zspec[plane * 8 + i])
            out_features[i * 8:(i + 1) * 8, plane] = lines.reshape(8, 32, 128).astype(BF)

    get_widen.wait()
    receive(X_D_CORE, 0, dc_in)
    mine = dy_in[:, ours].reshape(256, 128)
    far = dc_in[...].reshape(256, 128)
    y_taps = y_taps.reshape(2, 2, 8, 128)
    y_mine = jnp.where(half == 0, y_taps[:, 0], y_taps[:, 1]).reshape(16, 1, 128)
    y_far = jnp.where(half == 0, y_taps[:, 1], y_taps[:, 0]).reshape(16, 1, 128)
    for r in range(RX):
        wide = widen[:, r * 128:(r + 1) * 128]
        total = dot(mine, wide).reshape(16, 16, 128) * y_mine + dot(far, wide).reshape(16, 16, 128) * y_far
        out_core[:, r * 128:(r + 1) * 128] = jnp.sum(total, axis=0)[:9]

    receive(X_F_CORE, 0, fc_in)
    out_modes[...] = fc_out[...] + fc_in[...]
    receive(X_G_CORE, 0, gc_in)
    for which, sums in ((half, gc_out[...]), (1 - half, gc_in[...])):
        out_pair[which] = jnp.concatenate([sums[:, :C], sums[:, C:]], axis=0)
    for copy in sends:
        copy.wait_send()


def write_out(planes, core_rows, pair, modes, features, core, g_in, g_out, g_x, g_y, g_z, x_v, y_v, z_v, sem):
    copies = [pltpu.make_async_copy(planes.at[i * 32:(i + 1) * 32], features.at[i * 32:(i + 1) * 32], sem.at[i]) for i in range(2)]
    copies.append(pltpu.make_async_copy(core_rows, core, sem.at[2]))
    copies.append(pltpu.make_async_copy(pair.at[0], g_in, sem.at[3]))
    copies.append(pltpu.make_async_copy(pair.at[1], g_out, sem.at[4]))
    for copy in copies:
        copy.start()
    x_v[...] = modes[:, 0:32]
    y_v[...] = modes[:, 32:64]
    z_v[...] = modes[0:8, 64:80]
    for i, (src, dst) in enumerate(((x_v, g_x), (y_v, g_y), (z_v, g_z))):
        copies.append(pltpu.make_async_copy(src, dst, sem.at[5 + i]))
        copies[-1].start()
    for copy in copies:
        copy.wait()


def shards(features, cotangent, tucker_core, in_factor, out_factor, x_factor, y_factor, z_factor):
    tables = [jnp.asarray(m) for m in constants()]
    hbm = pl.BlockSpec(memory_space=pltpu.HBM)
    vmem = pl.BlockSpec(memory_space=pltpu.VMEM)
    buffers = [
        ((2, 64, 2, 32, 128), BF), ((2304, 2048), BF), ((48, 64), F32), ((48, 64), F32), ((16, 32), F32),
        ((16, 32), F32), ((8, 16), F32),
        ((256, 256), BF), ((256, 256), BF), ((32, 128), BF), ((128, 1024), BF), ((2, 128, 128), BF),
        ((256, 128), BF), ((128, 256), BF), ((128, 128), BF), ((512, 384), BF), ((128, 2048), BF),
        ((32, 256, 128), BF), ((4, 8, 16, 256), BF), ((2, 8, 16, 256), BF), ((16, 16, 256), BF), ((16, 16, 256), BF),
        ((8, 16, 256), BF), ((8, 16, 256), BF),
        ((64, 2048), BF), ((2304, 64), F32), ((8, 384, 64), BF), ((8, 32, 384), BF), ((8, 32, 384), BF),
        ((48, 48, 64), F32), ((8, 16, 128), BF), ((8, 16, 128), BF),
        ((2, 24, 128), F32), ((24, 128), F32), ((24, 128), F32), ((8, 24, 128), F32), ((24, 128), F32),
        ((4, 24, 128), F32), ((24, 128), F32), ((4, 24, 128), F32), ((24, 128), F32), ((24, 128), F32),
        ((16, 128), F32), ((8, 16, 128), F32), ((16, 128), F32), ((4, 16, 128), F32), ((16, 128), F32),
        ((4, 16, 128), F32), ((16, 128), F32), ((16, 128), F32),
        ((16, 32, 128), BF), ((16, 32, 128), BF), ((16, 16, 128), BF), ((8, 16, 128), BF), ((2, 16, 16, 128), BF),
        ((16, 256, 128), BF),
    ]
    factors = (in_factor, out_factor, x_factor, y_factor, z_factor)
    operands = [features, cotangent, tucker_core] + [a.T for a in factors] + tables
    results = pl.pallas_call(
        kernel,
        out_shape=(
            pltpu.VMEM((C, 2, 32, NZ), BF),
            pltpu.VMEM((9, 2048), F32),
            pltpu.VMEM((2, RIN, C), F32),
            pltpu.VMEM((16, 128), F32),
        ),
        in_specs=[hbm] * (8 + len(tables)),
        out_specs=(vmem, vmem, vmem, vmem),
        scratch_shapes=[pltpu.VMEM(shape, dtype) for shape, dtype in buffers] + [
            pltpu.SemaphoreType.DMA((28,)),
            pltpu.SemaphoreType.DMA((18, 16)),
            pltpu.SemaphoreType.DMA((18, 16)),
        ],
        compiler_params=pltpu.CompilerParams(
            collective_id=0, has_side_effects=True, vmem_limit_bytes=32 * 1024 * 1024
        ),
    )(*[pltpu.with_memory_space_constraint(a, pltpu.HBM) for a in operands])
    outs = pl.pallas_call(
        write_out,
        out_shape=(
            jax.ShapeDtypeStruct((C, 2, 32, NZ), BF),
            jax.ShapeDtypeStruct((9, 2048), F32),
            jax.ShapeDtypeStruct((RIN, C), F32),
            jax.ShapeDtypeStruct((ROUT, C), F32),
            jax.ShapeDtypeStruct((RX, KX), F32),
            jax.ShapeDtypeStruct((RY, KY), F32),
            jax.ShapeDtypeStruct((RZ, KZ), F32),
        ),
        in_specs=[vmem] * 4,
        out_specs=[hbm] * 7,
        scratch_shapes=[
            pltpu.VMEM((RX, KX), F32), pltpu.VMEM((RY, KY), F32), pltpu.VMEM((RZ, KZ), F32),
            pltpu.SemaphoreType.DMA((8,)),
        ],
    )(*[pltpu.with_memory_space_constraint(a, pltpu.VMEM) for a in results])
    return outs[0], outs[1], outs[2].T, outs[3].T, outs[4].T, outs[5].T, outs[6].T


def solution(mesh):
    placed = (P(None, "px", "py", None), P(None, "px", "py", None), P(), P(), P(), P(), P(), P())
    return jax.shard_map(
        shards,
        mesh=mesh,
        in_specs=placed,
        out_specs=(P(None, "px", "py", None), P(("px", "py"), None), P(), P(), P(), P(), P()),
        check_vma=False,
    )
```

time: 55 us -> 48.2 us (0.88)
  Pallas kernels: 52 us -> 47.4 us
  local copies, waits for them, and re-layouts: 2.23 us -> 0 us
    pallas_call x1, Pallas kernels: 49.6 us -> 46.3 us  [shards(): pl.pallas_call(kernel, out_shape=(pltpu.VMEM((C, 2, 32, NZ), BF), pltpu.V...]
    unnamed x6 -> x0, local copies, waits for them, and re-layouts: 2.23 us -> none
    pallas_call x1, Pallas kernels: 2.38 us -> 1.09 us  [shards(): pl.pallas_call(write_out, out_shape=(jax.ShapeDtypeStruct((C, 2, 32, NZ),...]
where the time goes in v2:
time: 48.2 us; the launch traced here: 48.1 us
  Pallas kernels  47.4 us (98%)
  between operations  0.64 us (1%)
    pallas_call x1, Pallas kernels, shards(): pl.pallas_call(kernel, out_shape=(pltpu.VMEM((C, 2, 32, NZ), BF), pltpu.V...  46.3 us
    pallas_call x1, Pallas kernels, shards(): pl.pallas_call(write_out, out_shape=(jax.ShapeDtypeStruct((C, 2, 32, NZ),...  1.09 us

profile of v2, /device:TPU:1, one launch (start us, length us, event | category | flops | bytes accessed | tf_op | source)
XLA Modules:
  0.0 48.1 jit_solution(14688031201303424890)
XLA Ops:
  0.6 46.3 %shard_map.225 = (bf16[64,2,32,128]{3,2,1,0:T(8,128)(2,1)S(1)}, f32[9,2048]{1,0:T(8,128)S(1)}, f32[2,48,64]{2,1,0:T(8,128)S(1)}, f32[16,128]{1,0:T(8,128)S(1)}) custom-call(bf16[64,2,32,128]{3,2,1,0:T(8,128)(2,1)} %feat.1, bf16[64,2,32,128]{3,2,1,0:T(8,128)(2,1)} %cot.1, bf16[2304,2048]{1,0:T(8,128)(2,1)} %core.1, f32[48,64]{1,0:T(8,128)} %bitcast.10, ...), custom_call_target="tpu_custom_call" | custom-call | tf_op jit(solution)/shard_map/pallas_call | solution.py:477
  47.0 1.1 %shard_map.226 = (bf16[64,2,32,128]{3,2,1,0:T(8,128)(2,1)}, f32[9,2048]{1,0:T(8,128)}, f32[48,64]{1,0:T(8,128)}, f32[48,64]{1,0:T(8,128)}, f32[16,32]{1,0:T(8,128)}, /*index=5*/f32[16,32]{1,0:T(8,128)}, f32[8,16]{1,0:T(8,128)}) custom-call(bf16[64,2,32,128]{3,2,1,0:T(8,128)(2,1)S(1)} %get-tuple-element.18.planes, f32[9,2048]{1,0:T(8,128)S(1)} %get-tuple-element.19.core_rows, ...), custom_call_target="tpu_custom_call" | custom-call | tf_op jit(solution)/shard_map/pallas_call | solution.py:496

commit v3 on v2

--- a/solution.py
+++ b/solution.py
@@ -87,8 +87,8 @@
 
 (
     X_A_CORE, X_A_XY, X_A_Z, X_D_Z, X_C_Z, X_D_XY, X_C_XY, X_D_CORE, X_C_CORE,
-    X_G_SPLIT, X_G_Z, X_G_X, X_G_Y, X_G_CORE, X_F_Z, X_F_X, X_F_Y, X_F_CORE,
-) = range(18)
+    X_G_SPLIT, X_G_Z, X_G_XY, X_G_CORE,
+) = range(13)
 
 
 def iota(shape, dim):
@@ -111,8 +111,7 @@
     fwd, bwd, zrows, zblock, gather, spread, swap, swapt, rows9, widen,
     yspec, part, core_in, a_out, a_in, az_out, az_in,
     modes, uvt, uvp, d_out, d_in, w_all, c_out, c_in,
-    g_out, gs_in, gz_out, gz_in, gx_out, gx_in, gy_out, gy_in, gc_out, gc_in,
-    f_out, fz_in, fx_out, fx_in, fy_out, fy_in, fc_out, fc_in,
+    g_out, gs_in, gz_out, gz_in, gx_out, gx_in, gc_out, gc_in,
     dy_out, dy_in, dc_in, cy_out, cp_in,
     zspec, local_sem, send_sem, recv_sem,
 ):
@@ -135,15 +134,7 @@
         there = lax.rem(other, 8)
         return (there // 4 * 32 + z * 4 + lax.rem(there, 4), other // 8 * 2 + half)
 
-    def at_x(other):
-        return (y_lo * 32 + z * 4 + other, py)
-
-    def at_y(other):
-        return (lax.rem(other, 2) * 32 + z * 4 + x4, other // 2 * 2 + half)
-
     along_z = [lax.rem(z + d, 8) for d in (4, 3, 5, 2, 6, 1, 7)]
-    along_x = [lax.rem(x4 + d, 4) for d in (2, 1, 3)]
-    along_y = [lax.rem(y + d, 4) for d in (2, 1, 3)]
     along_xy = [
         lax.rem(y + dy, 4) * 4 + lax.rem(x4 + dx, 4)
         for dy, dx in (
@@ -185,30 +176,28 @@
     get_bwd = load(k_bwd.at[py], bwd)
     get_widen = load(k_widen, widen)
 
-    sends = []
-
-    def send(number, slot_out, slot_in, src, dst, device):
-        copy = pltpu.make_async_remote_copy(
-            src_ref=src, dst_ref=dst, send_sem=send_sem.at[number, slot_out],
-            recv_sem=recv_sem.at[number, slot_in], device_id=device, device_id_type=MESH,
+    sent = []
+
+    def descriptor(number, src, dst, device):
+        return pltpu.make_async_remote_copy(
+            src_ref=src, dst_ref=dst, send_sem=send_sem.at[number], recv_sem=recv_sem.at[number],
+            device_id=device, device_id_type=MESH,
         )
+
+    def swap_cores(number, src, dst):
+        copy = descriptor(number, src, dst, other_core)
         copy.start()
-        sends.append(copy)
-
-    def receive(number, slot, dst):
-        pltpu.make_async_remote_copy(
-            src_ref=dst, dst_ref=dst, send_sem=send_sem.at[number, slot],
-            recv_sem=recv_sem.at[number, slot], device_id=other_core, device_id_type=MESH,
-        ).wait_recv()
+        sent.append(copy)
+        return copy
 
     def exchange(number, src_of, into, mine, others, device_of):
-        for d, other in enumerate(others):
-            send(number, d, mine, src_of(other), into.at[mine], device_of(other))
+        for other in others:
+            descriptor(number, src_of(other), into.at[mine], device_of(other)).start()
         into[mine] = src_of(mine)[...]
-
-    def arrive(number, into, others):
-        for other in others[::-1]:
-            receive(number, other, into.at[other])
+        blocks = into.at[0:len(others)]
+        whole = descriptor(number, blocks, blocks, other_core)
+        sent.append(whole)
+        return whole
 
     get_fwd.wait()
     for i in range(4):
@@ -228,26 +217,24 @@
             lax.fori_loop(0, 2, lines, 0, unroll=True)
     get_zrows.wait()
 
-    def depth(group):
+    def depth(c, h):
         def one(i, carry):
-            both = dot(zrows[...], yspec[group * 8 + i], NT)
-            part[group, i] = (both[:KZ] + both[KZ:]).astype(BF)
+            both = dot(zrows[...], yspec[(h * 2 + c) * 8 + i], NT)
+            part[c, h * 8 + i] = (both[:KZ] + both[KZ:]).astype(BF)
             return carry
 
         lax.fori_loop(0, 8, one, 0, unroll=4)
 
     for h in range(2):
-        depth(h * 2 + (1 - half))
+        depth(1 - half, h)
     pl.semaphore_wait(barrier, 23)
+    a_core = swap_cores(X_A_CORE, part.at[1 - half], core_in)
     for h in range(2):
-        send(X_A_CORE, h, h, part.at[h * 2 + (1 - half)], core_in.at[h], other_core)
-    for h in range(2):
-        depth(h * 2 + half)
-
-    for h in range(2):
-        receive(X_A_CORE, h, core_in.at[h])
-        a_out[h * 8:(h + 1) * 8] = (part[h * 2 + half].astype(F32) + core_in[h].astype(F32)).astype(BF)
-    exchange(X_A_XY, lambda o: a_out.at[o], a_in, xy, along_xy, at_xy)
+        depth(half, h)
+
+    a_core.wait_recv()
+    a_out[...] = (part[half].astype(F32) + core_in[...].astype(F32)).astype(BF)
+    a_xy = exchange(X_A_XY, lambda o: a_out.at[o], a_in, xy, along_xy, at_xy)
 
     for copy in get_small:
         copy.wait()
@@ -280,16 +267,16 @@
             uvp[block, m * 192 + 144:(m + 1) * 192, :] = jnp.zeros((48, 64), BF)
 
     get_swap.wait()
-    arrive(X_A_XY, a_in, along_xy)
+    a_xy.wait_recv()
     az_out[...] = dot(swap[...], a_in[...].reshape(256, 256)).astype(BF).reshape(8, 16, 256)
-    exchange(X_A_Z, lambda o: az_out.at[o], az_in, z, along_z, at_z)
+    a_z = exchange(X_A_Z, lambda o: az_out.at[o], az_in, z, along_z, at_z)
 
     get_core.wait()
     for g in range(8):
         w_all[g * 6:(g + 1) * 6] = dot(core_v[g * 288:(g + 1) * 288, :], modes[...], NT).reshape(6, 48, 64)
 
     get_gather.wait()
-    arrive(X_A_Z, az_in, along_z)
+    a_z.wait_recv()
     slabs = az_in[...].reshape(128, 256)
     both = dot(gather[0], slabs[:, :128]) + dot(gather[1], slabs[:, 128:])
     spec = both[:64] + both[64:]
@@ -305,7 +292,7 @@
     for g in range(8):
         flow = dot(x_parts, uvp[g], NT)
         d_out[g] = (flow[:32] + flow[32:]).astype(BF)
-    exchange(X_D_Z, lambda o: d_out.at[o], d_in, z, along_z, at_z)
+    d_z = exchange(X_D_Z, lambda o: d_out.at[o], d_in, z, along_z, at_z)
 
     weight = w_all[...]
     h_t = jnp.sum(weight * v_t[None, :, :], axis=1)
@@ -317,13 +304,12 @@
     get_spread.wait()
     synth = dot(spread[...], pulled)
     c_out[...] = (synth[:128] + synth[128:]).astype(BF).reshape(8, 16, 128)
-    exchange(X_C_Z, lambda o: c_out.at[o], c_in, z, along_z, at_z)
+    c_z = exchange(X_C_Z, lambda o: c_out.at[o], c_in, z, along_z, at_z)
 
     g_t = jnp.sum(weight * u_t[:, None, :], axis=0)
     for f, ranks in enumerate((h_t, g_t)):
         grad = dot(ranks, spec[:, f * C:(f + 1) * C], NN, EXACT)
-        g_out[f] = jnp.concatenate([grad[:24], grad[24:]], axis=1)
-    send(X_G_SPLIT, 0, 0, g_out.at[1 - half], gs_in, other_core)
+        g_out[f, :24] = jnp.concatenate([grad[:24], grad[24:]], axis=1)
 
     uv = uvt[...].T.astype(BF)
     x_sum = jnp.zeros((64, 128), F32)
@@ -350,44 +336,35 @@
     for n in range(2):
         z_col = jnp.sum(z_pick * jnp.sum(z_sum[n * 32:(n + 1) * 32], axis=0, keepdims=True), axis=1, keepdims=True)
         modes_grad = modes_grad + jnp.where(lane16 == 64 + 2 * z + n, z_col, 0.0)
-    f_out[...] = modes_grad
-    exchange(X_F_Z, lambda o: f_out, fz_in, z, along_z, at_z)
-
-    receive(X_G_SPLIT, 0, gs_in)
-    gz_out[...] = g_out[half] + gs_in[...]
-    exchange(X_G_Z, lambda o: gz_out, gz_in, z, along_z, at_z)
-
-    arrive(X_D_Z, d_in, along_z)
+    for f in range(2):
+        g_out[f, 24:] = modes_grad[f * 8:(f + 1) * 8]
+    g_split = swap_cores(X_G_SPLIT, g_out.at[1 - half], gs_in)
+    g_split.wait_recv()
+    gz_out[...] = (g_out[half] + gs_in[...]).astype(BF)
+    g_z = exchange(X_G_Z, lambda o: gz_out, gz_in, z, along_z, at_z)
+
+    d_z.wait_recv()
     taps = dot(d_in[...].reshape(256, 384), z_parts, TN)
     taps = (taps[:, :128] + taps[:, 128:]).astype(BF)
     get_rows9.wait()
     dy_out[...] = dot(rows9[...], taps).astype(BF).reshape(16, 32, 128)
-    exchange(X_D_XY, lambda o: dy_out.at[o], dy_in, xy, along_xy, at_xy)
+    d_xy = exchange(X_D_XY, lambda o: dy_out.at[o], dy_in, xy, along_xy, at_xy)
 
     get_swapt.wait()
-    arrive(X_C_Z, c_in, along_z)
+    c_z.wait_recv()
     cy_out[...] = dot(swapt[...], c_in[...].reshape(128, 128)).astype(BF).reshape(8, 16, 128)
-    exchange(X_C_XY, lambda o: cy_out.at[lax.rem(o, 8)], cp_in.at[half], xy, along_xy, at_xy)
-
-    arrive(X_F_Z, fz_in, along_z)
-    fx_out[...] = jnp.sum(fz_in[...], axis=0)
-    exchange(X_F_X, lambda o: fx_out, fx_in, x4, along_x, at_x)
-    arrive(X_G_Z, gz_in, along_z)
-    gx_out[...] = jnp.sum(gz_in[...], axis=0)
-    exchange(X_G_X, lambda o: gx_out, gx_in, x4, along_x, at_x)
-    arrive(X_F_X, fx_in, along_x)
-    fy_out[...] = jnp.sum(fx_in[...], axis=0)
-    exchange(X_F_Y, lambda o: fy_out, fy_in, y, along_y, at_y)
-    arrive(X_G_X, gx_in, along_x)
-    gy_out[...] = jnp.sum(gx_in[...], axis=0)
-    exchange(X_G_Y, lambda o: gy_out, gy_in, y, along_y, at_y)
-
-    arrive(X_C_XY, cp_in.at[half], along_xy)
-    send(X_C_CORE, 0, 0, cp_in.at[half], cp_in.at[half], other_core)
-    arrive(X_D_XY, dy_in, along_xy)
+    c_xy = exchange(X_C_XY, lambda o: cy_out.at[lax.rem(o, 8)], cp_in.at[half], xy, along_xy, at_xy)
+
+    g_z.wait_recv()
+    gx_out[...] = jnp.sum(gz_in[...].astype(F32), axis=0).astype(BF)
+    g_xy = exchange(X_G_XY, lambda o: gx_out, gx_in, xy, along_xy, at_xy)
+
+    c_xy.wait_recv()
+    c_core = swap_cores(X_C_CORE, cp_in.at[half], cp_in.at[half])
+    d_xy.wait_recv()
     theirs = pl.ds(pl.multiple_of((1 - half) * 16, 16), 16)
     ours = pl.ds(pl.multiple_of(half * 16, 16), 16)
-    send(X_D_CORE, 0, 0, dy_in.at[:, theirs], dc_in, other_core)
+    d_core = swap_cores(X_D_CORE, dy_in.at[:, theirs], dc_in)
 
     def deepen(group, modes_of):
         deep = dot(modes_of.reshape(128, 128), zblock[...], TN)
@@ -399,13 +376,7 @@
     get_zblock.wait()
     for h in range(2):
         deepen(h * 2 + half, cp_in[half, h * 8:(h + 1) * 8])
-    arrive(X_F_Y, fy_in, along_y)
-    fc_out[...] = jnp.sum(fy_in[...], axis=0)
-    send(X_F_CORE, 0, 0, fc_out, fc_in, other_core)
-    arrive(X_G_Y, gy_in, along_y)
-    gc_out[...] = jnp.sum(gy_in[...], axis=0)
-    send(X_G_CORE, 0, 0, gc_out, gc_in, other_core)
-    receive(X_C_CORE, 0, cp_in.at[1 - half])
+    c_core.wait_recv()
     for h in range(2):
         deepen(h * 2 + 1 - half, cp_in[1 - half, h * 8:(h + 1) * 8])
     get_bwd.wait()
@@ -415,7 +386,7 @@
             out_features[i * 8:(i + 1) * 8, plane] = lines.reshape(8, 32, 128).astype(BF)
 
     get_widen.wait()
-    receive(X_D_CORE, 0, dc_in)
+    d_core.wait_recv()
     mine = dy_in[:, ours].reshape(256, 128)
     far = dc_in[...].reshape(256, 128)
     y_taps = y_taps.reshape(2, 2, 8, 128)
@@ -426,12 +397,14 @@
         total = dot(mine, wide).reshape(16, 16, 128) * y_mine + dot(far, wide).reshape(16, 16, 128) * y_far
         out_core[:, r * 128:(r + 1) * 128] = jnp.sum(total, axis=0)[:9]
 
-    receive(X_F_CORE, 0, fc_in)
-    out_modes[...] = fc_out[...] + fc_in[...]
-    receive(X_G_CORE, 0, gc_in)
+    g_xy.wait_recv()
+    gc_out[...] = jnp.sum(gx_in[...].astype(F32), axis=0)
+    g_core = swap_cores(X_G_CORE, gc_out, gc_in)
+    g_core.wait_recv()
     for which, sums in ((half, gc_out[...]), (1 - half, gc_in[...])):
-        out_pair[which] = jnp.concatenate([sums[:, :C], sums[:, C:]], axis=0)
-    for copy in sends:
+        out_pair[which] = jnp.concatenate([sums[:24, :C], sums[:24, C:]], axis=0)
+        out_modes[which] = sums[24:]
+    for copy in sent:
         copy.wait_send()
 
 
@@ -442,9 +415,9 @@
     copies.append(pltpu.make_async_copy(pair.at[1], g_out, sem.at[4]))
     for copy in copies:
         copy.start()
-    x_v[...] = modes[:, 0:32]
-    y_v[...] = modes[:, 32:64]
-    z_v[...] = modes[0:8, 64:80]
+    x_v[...] = modes[...].reshape(16, 128)[:, 0:32]
+    y_v[...] = modes[...].reshape(16, 128)[:, 32:64]
+    z_v[...] = modes[0, :, 64:80]
     for i, (src, dst) in enumerate(((x_v, g_x), (y_v, g_y), (z_v, g_z))):
         copies.append(pltpu.make_async_copy(src, dst, sem.at[5 + i]))
         copies[-1].start()
@@ -461,14 +434,12 @@
         ((16, 32), F32), ((8, 16), F32),
         ((256, 256), BF), ((256, 256), BF), ((32, 128), BF), ((128, 1024), BF), ((2, 128, 128), BF),
         ((256, 128), BF), ((128, 256), BF), ((128, 128), BF), ((512, 384), BF), ((128, 2048), BF),
-        ((32, 256, 128), BF), ((4, 8, 16, 256), BF), ((2, 8, 16, 256), BF), ((16, 16, 256), BF), ((16, 16, 256), BF),
+        ((32, 256, 128), BF), ((2, 16, 16, 256), BF), ((16, 16, 256), BF), ((16, 16, 256), BF), ((16, 16, 256), BF),
         ((8, 16, 256), BF), ((8, 16, 256), BF),
         ((64, 2048), BF), ((2304, 64), F32), ((8, 384, 64), BF), ((8, 32, 384), BF), ((8, 32, 384), BF),
         ((48, 48, 64), F32), ((8, 16, 128), BF), ((8, 16, 128), BF),
-        ((2, 24, 128), F32), ((24, 128), F32), ((24, 128), F32), ((8, 24, 128), F32), ((24, 128), F32),
-        ((4, 24, 128), F32), ((24, 128), F32), ((4, 24, 128), F32), ((24, 128), F32), ((24, 128), F32),
-        ((16, 128), F32), ((8, 16, 128), F32), ((16, 128), F32), ((4, 16, 128), F32), ((16, 128), F32),
-        ((4, 16, 128), F32), ((16, 128), F32), ((16, 128), F32),
+        ((2, 32, 128), F32), ((32, 128), F32), ((32, 128), BF), ((8, 32, 128), BF), ((32, 128), BF),
+        ((16, 32, 128), BF), ((32, 128), F32), ((32, 128), F32),
         ((16, 32, 128), BF), ((16, 32, 128), BF), ((16, 16, 128), BF), ((8, 16, 128), BF), ((2, 16, 16, 128), BF),
         ((16, 256, 128), BF),
     ]
@@ -480,14 +451,14 @@
             pltpu.VMEM((C, 2, 32, NZ), BF),
             pltpu.VMEM((9, 2048), F32),
             pltpu.VMEM((2, RIN, C), F32),
-            pltpu.VMEM((16, 128), F32),
+            pltpu.VMEM((2, 8, 128), F32),
         ),
         in_specs=[hbm] * (8 + len(tables)),
         out_specs=(vmem, vmem, vmem, vmem),
         scratch_shapes=[pltpu.VMEM(shape, dtype) for shape, dtype in buffers] + [
-            pltpu.SemaphoreType.DMA((28,)),
-            pltpu.SemaphoreType.DMA((18, 16)),
-            pltpu.SemaphoreType.DMA((18, 16)),
+            pltpu.SemaphoreType.DMA((24,)),
+            pltpu.SemaphoreType.DMA((13,)),
+            pltpu.SemaphoreType.DMA((13,)),
         ],
         compiler_params=pltpu.CompilerParams(
             collective_id=0, has_side_effects=True, vmem_limit_bytes=32 * 1024 * 1024

time: 48.2 us -> 40.9 us (0.85)
  Pallas kernels: 47.4 us -> 40.2 us
    pallas_call x1, Pallas kernels: 46.3 us -> 39.1 us  [shards(): pl.pallas_call(kernel, out_shape=(pltpu.VMEM((C, 2, 32, NZ), BF), pltpu.V...]
where the time goes in v3:
time: 40.9 us
  Pallas kernels  40.2 us (98%)
  between operations  0.64 us (2%)
    pallas_call x1, Pallas kernels, shards(): pl.pallas_call(kernel, out_shape=(pltpu.VMEM((C, 2, 32, NZ), BF), pltpu.V...  39.1 us
    pallas_call x1, Pallas kernels, shards(): pl.pallas_call(write_out, out_shape=(jax.ShapeDtypeStruct((C, 2, 32, NZ),...  1.09 us

profile of v3, /device:TPU:1, one launch (start us, length us, event | category | flops | bytes accessed | tf_op | source)
XLA Modules:
  0.0 40.9 jit_solution(8728447823795657140)
XLA Ops:
  0.6 39.1 %shard_map.225 = (bf16[64,2,32,128]{3,2,1,0:T(8,128)(2,1)S(1)}, f32[9,2048]{1,0:T(8,128)S(1)}, f32[2,48,64]{2,1,0:T(8,128)S(1)}, f32[2,8,128]{2,1,0:T(8,128)S(1)}) custom-call(bf16[64,2,32,128]{3,2,1,0:T(8,128)(2,1)} %feat.1, bf16[64,2,32,128]{3,2,1,0:T(8,128)(2,1)} %cot.1, bf16[2304,2048]{1,0:T(8,128)(2,1)} %core.1, f32[48,64]{1,0:T(8,128)} %bitcast.10, ...), custom_call_target="tpu_custom_call" | custom-call | tf_op jit(solution)/shard_map/pallas_call | solution.py:448
  39.8 1.1 %shard_map.226 = (bf16[64,2,32,128]{3,2,1,0:T(8,128)(2,1)}, f32[9,2048]{1,0:T(8,128)}, f32[48,64]{1,0:T(8,128)}, f32[48,64]{1,0:T(8,128)}, f32[16,32]{1,0:T(8,128)}, /*index=5*/f32[16,32]{1,0:T(8,128)}, f32[8,16]{1,0:T(8,128)}) custom-call(bf16[64,2,32,128]{3,2,1,0:T(8,128)(2,1)S(1)} %get-tuple-element.18.planes, f32[9,2048]{1,0:T(8,128)S(1)} %get-tuple-element.19.core_rows, ...), custom_call_target="tpu_custom_call" | custom-call | tf_op jit(solution)/shard_map/pallas_call | solution.py:467

commit v4 on v3

--- a/solution.py
+++ b/solution.py
@@ -86,9 +86,9 @@
 
 
 (
-    X_A_CORE, X_A_XY, X_A_Z, X_D_Z, X_C_Z, X_D_XY, X_C_XY, X_D_CORE, X_C_CORE,
+    X_A_CORE, X_A_XY, X_A_Z, X_D_Z, X_C_Z, X_DC_XY, X_D_CORE, X_C_CORE,
     X_G_SPLIT, X_G_Z, X_G_XY, X_G_CORE,
-) = range(13)
+) = range(12)
 
 
 def iota(shape, dim):
@@ -110,9 +110,9 @@
     field, core_v, fin_v, fout_v, fx_v, fy_v, fz_v,
     fwd, bwd, zrows, zblock, gather, spread, swap, swapt, rows9, widen,
     yspec, part, core_in, a_out, a_in, az_out, az_in,
-    modes, uvt, uvp, d_out, d_in, w_all, c_out, c_in,
+    modes, x_wide, uvt, uvp, d_out, d_in, w_all, c_out, c_in,
     g_out, gs_in, gz_out, gz_in, gx_out, gx_in, gc_out, gc_in,
-    dy_out, dy_in, dc_in, cy_out, cp_in,
+    dc_out, dc_in, d_far, c_far,
     zspec, local_sem, send_sem, recv_sem,
 ):
     px = lax.axis_index("px")
@@ -220,7 +220,7 @@
     def depth(c, h):
         def one(i, carry):
             both = dot(zrows[...], yspec[(h * 2 + c) * 8 + i], NT)
-            part[c, h * 8 + i] = (both[:KZ] + both[KZ:]).astype(BF)
+            part[c, h * 8 + i] = both[:KZ] + both[KZ:]
             return carry
 
         lax.fori_loop(0, 8, one, 0, unroll=4)
@@ -233,7 +233,7 @@
         depth(half, h)
 
     a_core.wait_recv()
-    a_out[...] = (part[half].astype(F32) + core_in[...].astype(F32)).astype(BF)
+    a_out[...] = (part[half] + core_in[...]).astype(BF)
     a_xy = exchange(X_A_XY, lambda o: a_out.at[o], a_in, xy, along_xy, at_xy)
 
     for copy in get_small:
@@ -250,7 +250,11 @@
     yz_lane = y_lane * z_lane
     x_rep = dot(flag(iota((64, KX), 1) == lax.rem(iota((64, KX), 0), KX)), fx_v[...], NT, EXACT)
     for r in range(RX):
-        modes[:, r * 128:(r + 1) * 128] = (x_rep[:, r:r + 1] * yz_lane).astype(BF)
+        x_wide[:, r * 128:(r + 1) * 128] = jnp.broadcast_to(x_rep[:, r:r + 1], (64, 128))
+        column = x_wide[:, r * 128:(r + 1) * 128] * yz_lane
+        high = column.astype(BF)
+        modes[:64, r * 128:(r + 1) * 128] = high
+        modes[64:, r * 128:(r + 1) * 128] = (column - high.astype(F32)).astype(BF)
     x_cols = dot(fx_v[...], flag(lax.rem(iota((KX, 64), 1), KX) == iota((KX, 64), 0)), NN, EXACT)
     x_cols = jnp.concatenate([x_cols, x_cols], axis=0)
     x_cols = jnp.where(iota((32, 64), 0) // RX == iota((32, 64), 1) // KX, x_cols, 0.0)
@@ -273,7 +277,8 @@
 
     get_core.wait()
     for g in range(8):
-        w_all[g * 6:(g + 1) * 6] = dot(core_v[g * 288:(g + 1) * 288, :], modes[...], NT).reshape(6, 48, 64)
+        both = dot(core_v[g * 288:(g + 1) * 288, :], modes[...], NT)
+        w_all[g * 6:(g + 1) * 6] = (both[:, :64] + both[:, 64:]).reshape(6, 48, 64)
 
     get_gather.wait()
     a_z.wait_recv()
@@ -320,7 +325,7 @@
             r = g * 2 + h
             piece = flow[:, h * 128:(h + 1) * 128]
             x_sum = x_sum + jnp.where(lane == r, jnp.sum(piece * yz_lane, axis=1, keepdims=True), 0.0)
-            yz_sum = yz_sum + piece * x_rep[:, r:r + 1]
+            yz_sum = yz_sum + piece * x_wide[:, r * 128:(r + 1) * 128]
     row16 = iota((16, 128), 0)
     lane16 = iota((16, 128), 1)
     modes_grad = dot(
@@ -347,24 +352,24 @@
     taps = dot(d_in[...].reshape(256, 384), z_parts, TN)
     taps = (taps[:, :128] + taps[:, 128:]).astype(BF)
     get_rows9.wait()
-    dy_out[...] = dot(rows9[...], taps).astype(BF).reshape(16, 32, 128)
-    d_xy = exchange(X_D_XY, lambda o: dy_out.at[o], dy_in, xy, along_xy, at_xy)
+    dc_out[:, :32] = dot(rows9[...], taps).astype(BF).reshape(16, 32, 128)
 
     get_swapt.wait()
     c_z.wait_recv()
-    cy_out[...] = dot(swapt[...], c_in[...].reshape(128, 128)).astype(BF).reshape(8, 16, 128)
-    c_xy = exchange(X_C_XY, lambda o: cy_out.at[lax.rem(o, 8)], cp_in.at[half], xy, along_xy, at_xy)
+    planes = dot(swapt[...], c_in[...].reshape(128, 128)).astype(BF).reshape(8, 16, 128)
+    for h in range(2):
+        dc_out[h * 8:(h + 1) * 8, 32:] = planes
+    dc_xy = exchange(X_DC_XY, lambda o: dc_out.at[o], dc_in, xy, along_xy, at_xy)
 
     g_z.wait_recv()
     gx_out[...] = jnp.sum(gz_in[...].astype(F32), axis=0).astype(BF)
     g_xy = exchange(X_G_XY, lambda o: gx_out, gx_in, xy, along_xy, at_xy)
 
-    c_xy.wait_recv()
-    c_core = swap_cores(X_C_CORE, cp_in.at[half], cp_in.at[half])
-    d_xy.wait_recv()
+    dc_xy.wait_recv()
     theirs = pl.ds(pl.multiple_of((1 - half) * 16, 16), 16)
     ours = pl.ds(pl.multiple_of(half * 16, 16), 16)
-    d_core = swap_cores(X_D_CORE, dy_in.at[:, theirs], dc_in)
+    c_core = swap_cores(X_C_CORE, dc_in.at[:, 32:48], c_far)
+    d_core = swap_cores(X_D_CORE, dc_in.at[:, theirs], d_far)
 
     def deepen(group, modes_of):
         deep = dot(modes_of.reshape(128, 128), zblock[...], TN)
@@ -375,27 +380,31 @@
 
     get_zblock.wait()
     for h in range(2):
-        deepen(h * 2 + half, cp_in[half, h * 8:(h + 1) * 8])
+        deepen(h * 2 + half, dc_in[h * 8:(h + 1) * 8, 32:])
+    get_widen.wait()
+    y_taps = y_taps.reshape(2, 2, 8, 128)
+    y_mine = jnp.where(half == 0, y_taps[:, 0], y_taps[:, 1]).reshape(16, 1, 128)
+    y_far = jnp.where(half == 0, y_taps[:, 1], y_taps[:, 0]).reshape(16, 1, 128)
+
+    def core_part(rows, weights, first):
+        for r in range(RX):
+            cols = slice(r * 128, (r + 1) * 128)
+            wide = dot(rows, widen[:, cols]).reshape(16, 16, 128) * weights
+            part_sum = jnp.sum(wide, axis=0)[:9]
+            out_core[:, cols] = part_sum if first else out_core[:, cols] + part_sum
+
+    core_part(dc_in[:, ours].reshape(256, 128), y_mine, True)
     c_core.wait_recv()
     for h in range(2):
-        deepen(h * 2 + 1 - half, cp_in[1 - half, h * 8:(h + 1) * 8])
+        deepen(h * 2 + 1 - half, c_far[h * 8:(h + 1) * 8])
     get_bwd.wait()
     for plane in range(2):
         for i in range(8):
             lines = dot(bwd[...], zspec[plane * 8 + i])
             out_features[i * 8:(i + 1) * 8, plane] = lines.reshape(8, 32, 128).astype(BF)
 
-    get_widen.wait()
     d_core.wait_recv()
-    mine = dy_in[:, ours].reshape(256, 128)
-    far = dc_in[...].reshape(256, 128)
-    y_taps = y_taps.reshape(2, 2, 8, 128)
-    y_mine = jnp.where(half == 0, y_taps[:, 0], y_taps[:, 1]).reshape(16, 1, 128)
-    y_far = jnp.where(half == 0, y_taps[:, 1], y_taps[:, 0]).reshape(16, 1, 128)
-    for r in range(RX):
-        wide = widen[:, r * 128:(r + 1) * 128]
-        total = dot(mine, wide).reshape(16, 16, 128) * y_mine + dot(far, wide).reshape(16, 16, 128) * y_far
-        out_core[:, r * 128:(r + 1) * 128] = jnp.sum(total, axis=0)[:9]
+    core_part(d_far[...].reshape(256, 128), y_far, False)
 
     g_xy.wait_recv()
     gc_out[...] = jnp.sum(gx_in[...].astype(F32), axis=0)
@@ -434,13 +443,13 @@
         ((16, 32), F32), ((8, 16), F32),
         ((256, 256), BF), ((256, 256), BF), ((32, 128), BF), ((128, 1024), BF), ((2, 128, 128), BF),
         ((256, 128), BF), ((128, 256), BF), ((128, 128), BF), ((512, 384), BF), ((128, 2048), BF),
-        ((32, 256, 128), BF), ((2, 16, 16, 256), BF), ((16, 16, 256), BF), ((16, 16, 256), BF), ((16, 16, 256), BF),
+        ((32, 256, 128), BF), ((2, 16, 16, 256), F32), ((16, 16, 256), F32), ((16, 16, 256), BF), ((16, 16, 256), BF),
         ((8, 16, 256), BF), ((8, 16, 256), BF),
-        ((64, 2048), BF), ((2304, 64), F32), ((8, 384, 64), BF), ((8, 32, 384), BF), ((8, 32, 384), BF),
+        ((128, 2048), BF), ((64, 2048), F32), ((2304, 64), F32), ((8, 384, 64), BF), ((8, 32, 384), BF), ((8, 32, 384), BF),
         ((48, 48, 64), F32), ((8, 16, 128), BF), ((8, 16, 128), BF),
         ((2, 32, 128), F32), ((32, 128), F32), ((32, 128), BF), ((8, 32, 128), BF), ((32, 128), BF),
         ((16, 32, 128), BF), ((32, 128), F32), ((32, 128), F32),
-        ((16, 32, 128), BF), ((16, 32, 128), BF), ((16, 16, 128), BF), ((8, 16, 128), BF), ((2, 16, 16, 128), BF),
+        ((16, 48, 128), BF), ((16, 48, 128), BF), ((16, 16, 128), BF), ((16, 16, 128), BF),
         ((16, 256, 128), BF),
     ]
     factors = (in_factor, out_factor, x_factor, y_factor, z_factor)
@@ -457,8 +466,8 @@
         out_specs=(vmem, vmem, vmem, vmem),
         scratch_shapes=[pltpu.VMEM(shape, dtype) for shape, dtype in buffers] + [
             pltpu.SemaphoreType.DMA((24,)),
-            pltpu.SemaphoreType.DMA((13,)),
-            pltpu.SemaphoreType.DMA((13,)),
+            pltpu.SemaphoreType.DMA((12,)),
+            pltpu.SemaphoreType.DMA((12,)),
         ],
         compiler_params=pltpu.CompilerParams(
             collective_id=0, has_side_effects=True, vmem_limit_bytes=32 * 1024 * 1024

time: 40.9 us -> 41.4 us (1.012)
  Pallas kernels: 40.2 us -> 40.7 us
    pallas_call x1, Pallas kernels: 39.1 us -> 39.6 us  [shards(): pl.pallas_call(kernel, out_shape=(pltpu.VMEM((C, 2, 32, NZ), BF), pltpu.V...]
where the time goes in v4:
time: 41.4 us; the launch traced here: 41.3 us
  Pallas kernels  40.7 us (98%)
  between operations  0.64 us (2%)
    pallas_call x1, Pallas kernels, shards(): pl.pallas_call(kernel, out_shape=(pltpu.VMEM((C, 2, 32, NZ), BF), pltpu.V...  39.6 us
    pallas_call x1, Pallas kernels, shards(): pl.pallas_call(write_out, out_shape=(jax.ShapeDtypeStruct((C, 2, 32, NZ),...  1.09 us

profile of v4, /device:TPU:1, one launch (start us, length us, event | category | flops | bytes accessed | tf_op | source)
XLA Modules:
  0.0 41.3 jit_solution(12429911917038731265)
XLA Ops:
  0.6 39.6 %shard_map.225 = (bf16[64,2,32,128]{3,2,1,0:T(8,128)(2,1)S(1)}, f32[9,2048]{1,0:T(8,128)S(1)}, f32[2,48,64]{2,1,0:T(8,128)S(1)}, f32[2,8,128]{2,1,0:T(8,128)S(1)}) custom-call(bf16[64,2,32,128]{3,2,1,0:T(8,128)(2,1)} %feat.1, bf16[64,2,32,128]{3,2,1,0:T(8,128)(2,1)} %cot.1, bf16[2304,2048]{1,0:T(8,128)(2,1)} %core.1, f32[48,64]{1,0:T(8,128)} %bitcast.10, ...), custom_call_target="tpu_custom_call" | custom-call | tf_op jit(solution)/shard_map/pallas_call | solution.py:457
  40.3 1.1 %shard_map.226 = (bf16[64,2,32,128]{3,2,1,0:T(8,128)(2,1)}, f32[9,2048]{1,0:T(8,128)}, f32[48,64]{1,0:T(8,128)}, f32[48,64]{1,0:T(8,128)}, f32[16,32]{1,0:T(8,128)}, /*index=5*/f32[16,32]{1,0:T(8,128)}, f32[8,16]{1,0:T(8,128)}) custom-call(bf16[64,2,32,128]{3,2,1,0:T(8,128)(2,1)S(1)} %get-tuple-element.18.planes, f32[9,2048]{1,0:T(8,128)S(1)} %get-tuple-element.19.core_rows, ...), custom_call_target="tpu_custom_call" | custom-call | tf_op jit(solution)/shard_map/pallas_call | solution.py:476

commit v5 on v4

--- a/solution.py
+++ b/solution.py
@@ -220,7 +220,7 @@
     def depth(c, h):
         def one(i, carry):
             both = dot(zrows[...], yspec[(h * 2 + c) * 8 + i], NT)
-            part[c, h * 8 + i] = both[:KZ] + both[KZ:]
+            part[c, h * 8 + i] = (both[:KZ] + both[KZ:]).astype(BF)
             return carry
 
         lax.fori_loop(0, 8, one, 0, unroll=4)
@@ -233,7 +233,7 @@
         depth(half, h)
 
     a_core.wait_recv()
-    a_out[...] = (part[half] + core_in[...]).astype(BF)
+    a_out[...] = (part[half].astype(F32) + core_in[...].astype(F32)).astype(BF)
     a_xy = exchange(X_A_XY, lambda o: a_out.at[o], a_in, xy, along_xy, at_xy)
 
     for copy in get_small:
@@ -443,7 +443,7 @@
         ((16, 32), F32), ((8, 16), F32),
         ((256, 256), BF), ((256, 256), BF), ((32, 128), BF), ((128, 1024), BF), ((2, 128, 128), BF),
         ((256, 128), BF), ((128, 256), BF), ((128, 128), BF), ((512, 384), BF), ((128, 2048), BF),
-        ((32, 256, 128), BF), ((2, 16, 16, 256), F32), ((16, 16, 256), F32), ((16, 16, 256), BF), ((16, 16, 256), BF),
+        ((32, 256, 128), BF), ((2, 16, 16, 256), BF), ((16, 16, 256), BF), ((16, 16, 256), BF), ((16, 16, 256), BF),
         ((8, 16, 256), BF), ((8, 16, 256), BF),
         ((128, 2048), BF), ((64, 2048), F32), ((2304, 64), F32), ((8, 384, 64), BF), ((8, 32, 384), BF), ((8, 32, 384), BF),
         ((48, 48, 64), F32), ((8, 16, 128), BF), ((8, 16, 128), BF),

time: 41.4 us -> 40.8 us (0.986)
  Pallas kernels: 40.7 us -> 40.1 us
    pallas_call x1, Pallas kernels: 39.6 us -> 39 us  [shards(): pl.pallas_call(kernel, out_shape=(pltpu.VMEM((C, 2, 32, NZ), BF), pltpu.V...]
where the time goes in v5:
time: 40.8 us; the launch traced here: 40.7 us
  Pallas kernels  40.1 us (98%)
  between operations  0.64 us (2%)
    pallas_call x1, Pallas kernels, shards(): pl.pallas_call(kernel, out_shape=(pltpu.VMEM((C, 2, 32, NZ), BF), pltpu.V...  39 us
    pallas_call x1, Pallas kernels, shards(): pl.pallas_call(write_out, out_shape=(jax.ShapeDtypeStruct((C, 2, 32, NZ),...  1.09 us

profile of v5, /device:TPU:1, one launch (start us, length us, event | category | flops | bytes accessed | tf_op | source)
XLA Modules:
  0.0 40.7 jit_solution(6171742441991620705)
XLA Ops:
  0.6 39.0 %shard_map.225 = (bf16[64,2,32,128]{3,2,1,0:T(8,128)(2,1)S(1)}, f32[9,2048]{1,0:T(8,128)S(1)}, f32[2,48,64]{2,1,0:T(8,128)S(1)}, f32[2,8,128]{2,1,0:T(8,128)S(1)}) custom-call(bf16[64,2,32,128]{3,2,1,0:T(8,128)(2,1)} %feat.1, bf16[64,2,32,128]{3,2,1,0:T(8,128)(2,1)} %cot.1, bf16[2304,2048]{1,0:T(8,128)(2,1)} %core.1, f32[48,64]{1,0:T(8,128)} %bitcast.10, ...), custom_call_target="tpu_custom_call" | custom-call | tf_op jit(solution)/shard_map/pallas_call | solution.py:457
  39.7 1.1 %shard_map.226 = (bf16[64,2,32,128]{3,2,1,0:T(8,128)(2,1)}, f32[9,2048]{1,0:T(8,128)}, f32[48,64]{1,0:T(8,128)}, f32[48,64]{1,0:T(8,128)}, f32[16,32]{1,0:T(8,128)}, /*index=5*/f32[16,32]{1,0:T(8,128)}, f32[8,16]{1,0:T(8,128)}) custom-call(bf16[64,2,32,128]{3,2,1,0:T(8,128)(2,1)S(1)} %get-tuple-element.18.planes, f32[9,2048]{1,0:T(8,128)S(1)} %get-tuple-element.19.core_rows, ...), custom_call_target="tpu_custom_call" | custom-call | tf_op jit(solution)/shard_map/pallas_call | solution.py:476
